TPU v7x, 512 devices: a whole 4x8x8 slice. The times are simulated.
512 devices in a mesh: ctx: 64 (over y, z_lo, core), head: 8 (over z_hi, x).
Axes of the slice: x: 4, y: 8, z: 8 (z_hi: 2, z_lo: 4; z = z_hi * 4 + z_lo), core: 2. Of those that a mesh axis runs over, the one named last changes fastest.
Arguments:
- queries: bfloat16 [8192, 2048], P('ctx', 'head'), may hold values from -6 to 6
- keys: bfloat16 [8192, 2048], P('ctx', 'head'), may hold values from -6 to 6
- values: bfloat16 [8192, 2048], P('ctx', 'head'), may hold values from -6 to 6
- out_grad: bfloat16 [8192, 2048], P(('ctx', 'head')), may hold values from -6 to 6
Outputs:
- query_grad: bfloat16 [8192, 2048], P('ctx', 'head')
- key_grad: bfloat16 [8192, 2048], P('ctx', 'head')
- value_grad: bfloat16 [8192, 2048], P('ctx', 'head')
All inputs are finite; a program needn't handle non-finite values.
Results may differ from a plain program's by a relative error of at most 0.01.
Values may be sent and summed in bfloat16 or wider, within the bound.
No kernel may reach another device: no remote copies, remote signals or barrier semaphores. Data moves between devices by JAX's collectives and lax.ppermute only.
A program may use at most 64 MiB of HBM per device.

v0:
```python
import jax
import jax.numpy as jnp
from jax import lax
from jax.sharding import PartitionSpec as P

D_HEAD = 64


neg_fill = -1e30
score_block = 512


def masked_scores(query_part, key_part, query_first, key_first):
    scores = jnp.einsum(
        "qhd,khd->hqk", query_part, key_part, preferred_element_type=jnp.float32
    ) * D_HEAD ** (-0.5)
    query_pos = query_first + jnp.arange(query_part.shape[0])
    key_pos = key_first + jnp.arange(key_part.shape[0])
    allowed = key_pos[None, :] <= query_pos[:, None]
    return jnp.where(allowed[None], scores, neg_fill)


def shards(queries, keys, values, out_grad):
    tok_rows = queries.shape[0]
    width = queries.shape[1]
    num_heads = width // D_HEAD
    first = lax.axis_index("ctx") * tok_rows
    grad_local = lax.all_to_all(out_grad, "head", split_axis=1, concat_axis=0, tiled=True)
    key_all, value_all = (
        lax.all_gather(keys, "ctx", axis=0, tiled=True),
        lax.all_gather(values, "ctx", axis=0, tiled=True),
    )
    total_rows = key_all.shape[0]
    block = min(score_block, total_rows)
    count = (first + tok_rows - 1) // block + 1
    query_heads = queries.reshape(tok_rows, num_heads, D_HEAD)
    grad_heads = grad_local.reshape(tok_rows, num_heads, D_HEAD)
    key_heads = keys.reshape(tok_rows, num_heads, D_HEAD)
    value_heads = values.reshape(tok_rows, num_heads, D_HEAD)

    def key_slice(source, block_index):
        return lax.dynamic_slice_in_dim(source, block_index * block, block, 0).reshape(
            block, num_heads, D_HEAD
        )

    def stats_step(block_index, carry):
        top, exp_total = carry
        scores = masked_scores(
            query_heads, key_slice(key_all, block_index), first, block_index * block
        )
        new_top = jnp.maximum(top, jnp.max(scores, axis=2))
        rescale = jnp.exp(top - new_top)
        weights = jnp.exp(scores - new_top[:, :, None])
        exp_total = exp_total * rescale + jnp.sum(weights, axis=2)
        return (new_top, exp_total)

    zero_heads = jnp.zeros((tok_rows, num_heads, D_HEAD), jnp.float32)
    start_carry = (
        jnp.full((num_heads, tok_rows), neg_fill, jnp.float32),
        jnp.zeros((num_heads, tok_rows), jnp.float32),
    )
    top, exp_total = lax.fori_loop(0, count, stats_step, start_carry)
    log_total = top + jnp.log(exp_total)

    def output_step(block_index, acc_in):
        scores = masked_scores(
            query_heads, key_slice(key_all, block_index), first, block_index * block
        )
        probs_low = jnp.exp(scores - log_total[:, :, None]).astype(jnp.bfloat16)
        return acc_in + jnp.einsum(
            "hqk,khd->qhd",
            probs_low,
            key_slice(value_all, block_index),
            preferred_element_type=jnp.float32,
        )

    attn_out = lax.fori_loop(0, count, output_step, zero_heads)
    delta = jnp.sum(grad_heads.astype(jnp.float32) * attn_out, axis=2)

    def query_grad_step(block_index, acc_in):
        key_block = key_slice(key_all, block_index)
        value_block = key_slice(value_all, block_index)
        scores = masked_scores(query_heads, key_block, first, block_index * block)
        probs = jnp.exp(scores - log_total[:, :, None])
        dprobs = jnp.einsum(
            "qhd,khd->hqk", grad_heads, value_block, preferred_element_type=jnp.float32
        )
        dscores = (probs * (dprobs - delta.T[:, :, None])).astype(jnp.bfloat16)
        return acc_in + jnp.einsum(
            "hqk,khd->qhd", dscores, key_block, preferred_element_type=jnp.float32
        )

    query_total = lax.fori_loop(0, count, query_grad_step, zero_heads) * D_HEAD ** (-0.5)
    log_rows = log_total.T
    log_all, delta_all = (
        lax.all_gather(log_rows, "ctx", axis=0, tiled=True),
        lax.all_gather(delta, "ctx", axis=0, tiled=True),
    )
    query_piece = lax.all_gather(queries, "ctx", axis=0, tiled=True)
    grad_piece = lax.all_gather(grad_local, "ctx", axis=0, tiled=True)
    piece_rows = query_piece.shape[0]

    def inner_step(block_index, acc_in):
        row_start = block_index * score_block

        def work(acc_work):
            key_acc, value_acc = acc_work
            query_block = lax.dynamic_slice_in_dim(query_piece, row_start, score_block, 0).reshape(
                score_block, num_heads, D_HEAD
            )
            grad_block = lax.dynamic_slice_in_dim(grad_piece, row_start, score_block, 0).reshape(
                score_block, num_heads, D_HEAD
            )
            log_block = lax.dynamic_slice_in_dim(log_all, row_start, score_block, 0)
            delta_block = lax.dynamic_slice_in_dim(delta_all, row_start, score_block, 0)
            scores = masked_scores(query_block, key_heads, row_start, first)
            probs = jnp.exp(scores - log_block.T[:, :, None])
            probs_low = probs.astype(jnp.bfloat16)
            dprobs = jnp.einsum(
                "qhd,khd->hqk", grad_block, value_heads, preferred_element_type=jnp.float32
            )
            dscores = (probs * (dprobs - delta_block.T[:, :, None])).astype(jnp.bfloat16)
            key_acc = key_acc + jnp.einsum(
                "hqk,qhd->khd", dscores, query_block, preferred_element_type=jnp.float32
            )
            value_acc = value_acc + jnp.einsum(
                "hqk,qhd->khd", probs_low, grad_block, preferred_element_type=jnp.float32
            )
            return (key_acc, value_acc)

        def keep_same(acc_work):
            return acc_work

        return lax.cond(row_start + score_block - 1 >= first, work, keep_same, acc_in)

    key_total, value_total = lax.fori_loop(
        0, piece_rows // score_block, inner_step, (zero_heads, zero_heads)
    )
    key_total = key_total * D_HEAD ** (-0.5)
    return (
        query_total.reshape(tok_rows, width).astype(jnp.bfloat16),
        key_total.reshape(tok_rows, width).astype(jnp.bfloat16),
        value_total.reshape(tok_rows, width).astype(jnp.bfloat16),
    )


def solution(mesh):
    placed = (P("ctx", "head"), P("ctx", "head"), P("ctx", "head"), P(("ctx", "head"), None))
    return jax.shard_map(
        shards,
        mesh=mesh,
        in_specs=placed,
        out_specs=(P("ctx", "head"), P("ctx", "head"), P("ctx", "head")),
        check_vma=False,
    )
```

profile of v0, /device:TPU:1, one launch (start us, length us, event | category | flops | bytes accessed | tf_op | source)
XLA Modules:
  0.0 590.7 jit_solution(14808836722722370922)
XLA Ops:
  7.2 1.6 copy.51
  8.9 1.6 copy.53
  10.5 0.8 copy.70
  11.4 22.3 %all_to_all.19 = bf16[16,8,256]{2,0,1:T(8,128)(2,1)} all-to-all(bf16[16,8,256]{2,0,1:T(8,128)(2,1)S(1)} %bitcast.158), channel_id=1, replica_groups=mesh['ctx'=64,'head'=8] {'head'}, dimensions={1} | all-to-all | bytes 131072 | tf_op jit(solution)/shard_map/all_to_all | solution.py:28
  33.7 1.6 copy.52
  35.4 1.0 reshape.196
  36.4 104.1 %all-gather.5.cloned.1.call-done = bf16[8192,256]{0,1:T(8,128)(2,1)} async-done(((bf16[128,256]{0,1:T(8,128)(2,1)}), bf16[8192,256]{0,1:T(8,128)(2,1)}) %all-gather.5.cloned.1.call-update) | async-done | bytes 4194320 | tf_op jit(solution)/shard_map/all_gather | solution.py:30
  140.6 2.6 while.51
  140.6 1.0 constant_dynamic-slice_fusion.10
  141.7 1.2 fusion.71
  143.2 121.7 %all-gather.7.cloned.1.call-done = bf16[8192,256]{0,1:T(8,128)(2,1)} async-done(((bf16[128,256]{0,1:T(8,128)(2,1)}), bf16[8192,256]{0,1:T(8,128)(2,1)}) %all-gather.7.cloned.1.call-update) | async-done | bytes 4194320 | tf_op jit(solution)/shard_map/all_gather | solution.py:31
  264.8 2.7 while.52
  264.8 1.1 constant_dynamic-slice_fusion.11
  266.1 1.4 fusion.75
  268.0 3.0 while.53
  268.0 1.1 constant_dynamic-slice_fusion.12
  269.2 1.3 fusion.81
  271.0 0.7 copy.63
  271.8 180.3 %all_gather.23 = f32[8192,4]{1,0:T(8,128)} all-gather(f32[128,4]{1,0:T(8,128)S(1)} %multiply_reduce_fusion), channel_id=1, replica_groups=mesh['ctx'=64,'head'=8] {'ctx'}, dimensions={0}, use_global_device_ids=true | all-gather | bytes 133120 | tf_op jit(solution)/shard_map/all_gather | solution.py:97
  452.1 2.9 copy.62
  455.0 74.7 %all_gather.21 = f32[8192,4]{0,1:T(4,128)S(1)} all-gather(f32[128,4]{0,1:T(4,128)S(1)} %bitcast.161), channel_id=1, replica_groups=mesh['ctx'=64,'head'=8] {'ctx'}, dimensions={0}, use_global_device_ids=true | all-gather | bytes 133120 | tf_op jit(solution)/shard_map/all_gather | solution.py:96
  529.7 6.4 %copy.61 = bf16[8192,256]{0,1:T(8,128)(2,1)} copy(bf16[8192,256]{1,0:T(8,128)(2,1)} %all-gather.11.cloned.1.call-done) | data formatting | bytes 8388608 | tf_op jit(solution)/shard_map/while | solution.py:136
  536.2 46.5 %while.54 = (s32[]{:T(128)}, f32[128,4,64]{0,2,1:T(8,128)S(1)}, f32[128,4,64]{0,2,1:T(8,128)S(1)}, s32[]{:T(128)}, bf16[8192,256]{0,1:T(8,128)(2,1)}, /*index=5*...) while((s32[]{:T(128)}, f32[128,4,64]{0,2,1:T(8,128)S(1)}, ...), condition=%wide.region_12.13_spmd, body=%wide.region_9.12_spmd.sunk | while | flops 136184448 | bytes 6083925 | solution.py:136
  536.2 2.9 conditional.2
  536.2 1.1 constant_dynamic-slice_fusion.5
  539.1 2.9 conditional.2
  539.1 1.1 constant_dynamic-slice_fusion.5
  542.0 2.9 conditional.2
  542.0 1.1 constant_dynamic-slice_fusion.5
  543.3 0.7 fusion.30
  544.9 2.9 conditional.2
  544.9 1.1 constant_dynamic-slice_fusion.5
  546.2 0.7 fusion.30
  547.8 2.9 conditional.2
  547.8 1.1 constant_dynamic-slice_fusion.5
  549.1 0.7 fusion.30
  550.7 2.9 conditional.2
  550.7 1.1 constant_dynamic-slice_fusion.5
  553.6 2.9 conditional.2
  553.7 1.1 constant_dynamic-slice_fusion.5
  556.5 2.9 conditional.2
  556.6 1.1 constant_dynamic-slice_fusion.5
  557.8 0.7 fusion.30
  559.4 2.9 conditional.2
  559.5 1.1 constant_dynamic-slice_fusion.5
  560.7 0.7 fusion.30
  562.3 2.9 conditional.2
  562.4 1.1 constant_dynamic-slice_fusion.5
  565.3 2.9 conditional.2
  565.3 1.1 constant_dynamic-slice_fusion.5
  568.2 2.9 conditional.2
  568.2 1.1 constant_dynamic-slice_fusion.5
  571.1 2.9 conditional.2
  571.1 1.1 constant_dynamic-slice_fusion.5
  574.0 2.9 conditional.2
  574.0 1.1 constant_dynamic-slice_fusion.5
  575.2 0.7 fusion.30
  576.9 2.9 conditional.2
  576.9 1.1 constant_dynamic-slice_fusion.5
  578.2 0.7 fusion.30
  579.8 2.9 conditional.2
  579.8 1.1 constant_dynamic-slice_fusion.5
  582.7 0.7 copy.64
  583.5 0.7 copy.65
  (147 shorter events, 24.9 us)
Async XLA Ops:
  7.2 133.4 %all-gather.5.cloned.1.call-start = ((), (), s32[]{:S(2)}) async-start(), calls=%async_computation.1 | async-start | bytes 4259840 | tf_op jit(solution)/shard_map/all_gather | solution.py:30
  8.8 256.0 %all-gather.7.cloned.1.call-start = ((), (), s32[]{:S(2)}) async-start(), calls=%async_computation.2 | async-start | bytes 4259840 | tf_op jit(solution)/shard_map/all_gather | solution.py:31
  10.5 519.2 %all-gather.11.cloned.1.call-start = ((), (), s32[]{:S(2)}) async-start(), calls=%async_computation.4 | async-start | bytes 4259840 | tf_op jit(solution)/shard_map/all_gather | solution.py:100
  33.7 502.4 %all-gather.9.cloned.1.call-start = ((), (), s32[]{:S(2)}) async-start(), calls=%async_computation.3 | async-start | bytes 4259840 | tf_op jit(solution)/shard_map/all_gather | solution.py:99
  529.7 6.5 %copy-start = (bf16[128,256]{0,1:T(8,128)(2,1)S(1)}, bf16[128,256]{0,1:T(8,128)(2,1)}, u32[]{:S(2)}) copy-start(bf16[128,256]{0,1:T(8,128)(2,1)} %copy.53) | copy-start | bytes 196612
  529.7 6.5 %copy-start.1 = (bf16[128,256]{0,1:T(8,128)(2,1)S(1)}, bf16[128,256]{0,1:T(8,128)(2,1)}, u32[]{:S(2)}) copy-start(bf16[128,256]{0,1:T(8,128)(2,1)} %copy.51) | copy-start | bytes 196612
Sparse Core Ops, SparseCore 0:
  10.6 129.8 all-gather.4
  143.2 121.5 all-gather.6
  267.0 117.7 all-gather.10
  386.7 122.8 all-gather.8
where the time goes:
time: 595 us; the launch traced here: 591 us
  blocking collectives  277 us (47%)
  waiting for transfers between devices  226 us (38%)
  local copies, waits for them, and re-layouts  38.9 us (7%)
  matrix products  29.6 us (5%)
  between operations  13.9 us (2%)
    all_gather x1, blocking collectives, shards(): lax.all_gather(delta, 'ctx', axis=0, tiled=True)  180 us
    all_gather x1, waiting for transfers between devices, shards(): lax.all_gather(values, 'ctx', axis=0, tiled=True)  122 us
    all_gather x1, waiting for transfers between devices, shards(): lax.all_gather(keys, 'ctx', axis=0, tiled=True)  104 us
    all_gather x1, blocking collectives, shards(): lax.all_gather(log_rows, 'ctx', axis=0, tiled=True)  74.7 us
    all_to_all x1, blocking collectives, shards(): lax.all_to_all(out_grad, 'head', split_axis=1, concat_axis=0, tiled=True)  22.3 us
    dynamic_slice x16, local copies, waits for them, and re-layouts, work(): lax.dynamic_slice_in_dim(grad_piece, row_start, score_block, 0)  17.1 us
    dot_general x18, matrix products, masked_scores(): jnp.einsum('qhd,khd->hqk', query_part, key_part, preferred_element_type=j...  13.5 us
  transfers between devices with their start and end apart: 4, of which 2 were waited for; matrix products, arithmetic and copies ran while one was open for 4% of the time, Pallas kernels for 0%

commit v1 on v0

v1 whole, which is shorter than its diff:
```python
import functools

import jax
import jax.numpy as jnp
from jax import lax
from jax.experimental import pallas as pl
from jax.experimental.pallas import tpu as pltpu
from jax.sharding import Mesh
from jax.sharding import PartitionSpec as P

D_HEAD = 64
TOK = 128
GROUP = 4
SIDE = TOK * GROUP
SCALE = D_HEAD ** (-0.5)
EXP2_SCALE = SCALE * 1.4426950408889634
NEG = -1e30
FLOPS_PER_MICRO = 10**9
BF = jnp.bfloat16
F32 = jnp.float32

PART = TOK // GROUP
CHIPS = 32
HEADS = 8
PER = SIDE // PART // 2
HALF = SIDE // 2
QUAD = PER // 2
FULL = GROUP * (GROUP - 1) // 2


def chip_of(b, r1, c):
    return b * 8 + (c // 2) * 4 + r1 * 2 + c % 2


def call(body, out_shapes, scratch, *operands, micros=1, space=pltpu.VMEM, vmem=24):
    spaces = [pltpu.SMEM if x.dtype == jnp.int32 else space for x in operands]
    return pl.pallas_call(
        body,
        out_shape=out_shapes,
        in_specs=[pl.BlockSpec(memory_space=space) for space in spaces],
        out_specs=jax.tree.map(lambda _: pl.BlockSpec(memory_space=pltpu.VMEM), out_shapes),
        scratch_shapes=scratch,
        cost_estimate=pl.CostEstimate(
            flops=micros * FLOPS_PER_MICRO, bytes_accessed=2**20, transcendentals=0
        ),
        compiler_params=pltpu.CompilerParams(vmem_limit_bytes=vmem * 2**20),
    )(*operands)


def shape(*dims, dtype=BF):
    return jax.ShapeDtypeStruct(dims, dtype)


def split_grad(grad, out_ref):
    for g in range(HEADS):
        out_ref[g] = grad[:, g * GROUP * D_HEAD : (g + 1) * GROUP * D_HEAD]


def pack_body(at, q_ref, k_ref, v_ref, g_ref, out_ref, stage):
    core = at[2]
    for b in range(GROUP):
        lanes = slice(b * D_HEAD, (b + 1) * D_HEAD)
        both = jnp.concatenate([k_ref[:, lanes], v_ref[:, lanes]], axis=1)
        rows = jnp.concatenate([q_ref[:, lanes], g_ref[:, lanes]], axis=1)
        stage[...] = rows.reshape(GROUP, PART, 2 * D_HEAD)
        for r1 in range(2):
            keep, give = stage[2 * r1 + core], stage[2 * r1 + 1 - core]
            for c in range(GROUP):
                to = chip_of(b, r1, c)
                out_ref[to, :PART, :] = keep
                out_ref[to, PART : 2 * PART, :] = both[c * PART : (c + 1) * PART, :]
                out_ref[to, 2 * PART :, :] = give


def give_body(data, give_ref):
    give_ref[...] = data[:, PART:, :]


def make_bias(at):
    r, c, core = at[0], at[1], at[2]

    def block_start(index):
        block = 2 * ((index // PART) % QUAD) + (core ^ index // (HALF // 2))
        return block * TOK + index % PART

    key_pos = block_start(lax.broadcasted_iota(jnp.int32, (HALF, 1), 0)) + c * PART
    query_pos = block_start(lax.broadcasted_iota(jnp.int32, (1, HALF), 1)) + r * PART
    return jnp.where(key_pos <= query_pos, 0.0, NEG)


def mm(a, b):
    return lax.dot_general(a, b, (((1,), (0,)), ((), ())), preferred_element_type=F32)


def blocks(own, other, at):
    return jnp.concatenate(
        [
            ref[at * PER + half * QUAD : at * PER + (half + 1) * QUAD, first : first + PART, :]
            .reshape(HALF // 2, 2 * D_HEAD)
            for half in range(2)
            for ref, first in (own, other)
        ],
        axis=0,
    )


def row_block(data, other, u):
    return blocks((data, 0), (other, PART), u)


def col_block(data, other, v):
    return blocks((data, PART), (other, 0), v)


def below(v, u):
    return u * (u - 1) // 2 + v


def halves(both, axis):
    first = lax.broadcasted_iota(jnp.int32, both.shape, axis) < D_HEAD
    zeros = jnp.zeros_like(both)
    return jnp.where(first, both, zeros), jnp.where(first, zeros, both)


def stats_body(at, data, other, out_ref, *saved):
    s_tiles, dp_tiles = saved[:3], saved[3:]
    bias = make_bias(at)

    def multiply(u):
        q_low, g_low = halves(row_block(data, other, u).T, 0)
        kv_low = col_block(data, other, u)
        s = mm(kv_low[:HALF], q_low) * EXP2_SCALE
        s = jnp.concatenate([s[:, :HALF] + bias, s[:, HALF:]], axis=1)
        s_tiles[1][u] = s
        dp_tiles[1][u] = mm(kv_low[:HALF], g_low)
        top = jnp.max(s, axis=0, keepdims=True)
        yield None
        late = mm(kv_low[HALF:], q_low[:, HALF:]) * EXP2_SCALE + bias
        s_tiles[2][u] = late
        dp_tiles[2][u] = mm(kv_low[HALF:], g_low[:, HALF:])
        late_top = jnp.max(late, axis=0, keepdims=True)
        top = jnp.concatenate([top[:, :HALF], jnp.maximum(top[:, HALF:], late_top)], axis=1)
        yield top
        for v in range(u):
            kv_low = col_block(data, other, v)
            s = mm(kv_low, q_low) * EXP2_SCALE
            s_tiles[0][below(v, u)] = s
            dp_tiles[0][below(v, u)] = mm(kv_low, g_low)
            top = jnp.maximum(top, jnp.max(s, axis=0, keepdims=True))
            yield top

    def add_up(u, top):
        def sums(s, dp, top):
            p = jnp.exp2(s - top)
            return jnp.sum(p, axis=0, keepdims=True), jnp.sum(p * dp, axis=0, keepdims=True)

        first = sums(s_tiles[1][u], dp_tiles[1][u], top)
        yield None
        late = sums(s_tiles[2][u], dp_tiles[2][u], top[:, HALF:])
        total, weighted = (
            jnp.concatenate([a[:, :HALF], a[:, HALF:] + b], axis=1) for a, b in zip(first, late)
        )
        for v in range(u):
            yield None
            more = sums(s_tiles[0][below(v, u)], dp_tiles[0][below(v, u)], top)
            total, weighted = total + more[0], weighted + more[1]
        for d in range(GROUP):
            out_ref[d, u : u + 1, :] = top + jnp.log2(total)
            out_ref[d, u + GROUP : u + GROUP + 1, :] = weighted / total

    behind = iter(())
    for u in reversed(range(GROUP)):
        for top in multiply(u):
            next(behind, None)
        for _ in behind:
            pass
        behind = add_up(u, top)
    for _ in behind:
        pass


def grads_body(data, other, stats, *rest):
    s_tiles, dp_tiles, (dkv_ref, dq_ref, give_ref) = rest[:3], rest[3:6], rest[6:9]
    row_ref, q_rows, g_rows, dq_acc, dkv_acc = rest[9:]
    logs = [stats[d, :GROUP, :] for d in range(GROUP)]
    top = functools.reduce(jnp.maximum, logs)
    weights = [jnp.exp2(one - top) for one in logs]
    total = sum(weights)
    row_ref[:GROUP, :] = top + jnp.log2(total)
    row_ref[GROUP:, :] = sum(w * stats[d, GROUP:, :] for d, w in enumerate(weights)) / total
    for u in range(GROUP):
        q_rows[u], g_rows[u] = halves(row_block(data, other, u), 1)

    def probs_of(s, dp, u, lanes):
        p = jnp.exp2(s - row_ref[u : u + 1, lanes])
        ds = p * (dp - row_ref[GROUP + u : GROUP + u + 1, lanes])
        return p.astype(BF), ds.astype(BF)

    def both_grads(p, ds, u, lanes):
        return mm(ds, q_rows[u, lanes, :]) + mm(p, g_rows[u, lanes, :])

    late_lanes, lane = slice(HALF, SIDE), lax.broadcasted_iota(jnp.int32, (1, TOK), 1)
    factor = jnp.where(lane < D_HEAD, SCALE, 1.0)
    for v in range(GROUP):
        k_t = col_block(data, other, v).T[:D_HEAD, :]
        p, ds = probs_of(s_tiles[1][v], dp_tiles[1][v], v, slice(0, SIDE))
        dkv_acc[:HALF] = both_grads(p, ds, v, slice(0, SIDE))
        dq = mm(k_t[:, :HALF], ds)
        p, ds = probs_of(s_tiles[2][v], dp_tiles[2][v], v, late_lanes)
        dkv_acc[HALF:] = both_grads(p, ds, v, late_lanes)
        dq = jnp.concatenate([dq[:, :HALF], dq[:, HALF:] + mm(k_t[:, HALF:], ds)], axis=1)
        dq_acc[v] = dq if v == 0 else dq_acc[v] + dq
        for u in range(v + 1, GROUP):
            p, ds = probs_of(s_tiles[0][below(v, u)], dp_tiles[0][below(v, u)], u, slice(0, SIDE))
            dq = mm(k_t, ds)
            dq_acc[u] = dq if v == 0 else dq_acc[u] + dq
            dkv_acc[...] += both_grads(p, ds, u, slice(0, SIDE))
        done = (dkv_acc[...] * factor).astype(BF).reshape(2, 2, QUAD, PART, 2 * D_HEAD)
        for half in range(2):
            chips = slice(v * PER + half * QUAD, v * PER + (half + 1) * QUAD)
            dkv_ref[chips] = done[half, 0]
            give_ref[chips, :PART, :] = done[half, 1]
    for u in range(GROUP):
        dq = (dq_acc[u] * SCALE).T.astype(BF).reshape(2, 2, QUAD, PART, D_HEAD)
        dq = jnp.concatenate([dq[..., : PART // 2, :], dq[..., PART // 2 :, :]], axis=4)
        for half in range(2):
            chips = slice(u * PER + half * QUAD, u * PER + (half + 1) * QUAD)
            dq_ref[chips] = dq[half, 0]
            give_ref[chips, PART:, :] = dq[half, 1]


def pair_body(at, dkv, dq, got, out_ref):
    core = at[2]
    half = PART // 2
    out_ref[:, :PART, :] = (dkv[...].astype(F32) + got[:, :PART, :].astype(F32)).astype(BF)
    out_ref[:, pl.ds(pl.multiple_of(PART + core * half, half), half), :] = dq[...]
    out_ref[:, pl.ds(pl.multiple_of(PART + (1 - core) * half, half), half), :] = got[:, PART:, :]


def sum_body(part, dq_ref, dk_ref, dv_ref):
    def cols_of(b, c):
        return sum(part[chip_of(b, r1, c), :PART, :].astype(F32) for r1 in range(2))

    def rows_of(b, r):
        lines = slice(PART + (r % 2) * (PART // 2), PART + (r % 2 + 1) * (PART // 2))
        both = sum(part[chip_of(b, r // 2, c), lines, :].astype(F32) for c in range(GROUP))
        return jnp.concatenate([both[:, :D_HEAD], both[:, D_HEAD:]], axis=0)

    for pair in range(2):
        lanes = slice(pair * 2 * D_HEAD, (pair + 1) * 2 * D_HEAD)
        heads = (2 * pair, 2 * pair + 1)
        for x in range(GROUP):
            toks = slice(x * PART, (x + 1) * PART)
            dkv = [cols_of(b, x) for b in heads]
            dq_ref[toks, lanes] = jnp.concatenate([rows_of(b, x) for b in heads], axis=1).astype(BF)
            dk_ref[toks, lanes] = jnp.concatenate([a[:, :D_HEAD] for a in dkv], axis=1).astype(BF)
            dv_ref[toks, lanes] = jnp.concatenate([a[:, D_HEAD:] for a in dkv], axis=1).astype(BF)


CHIP_AXES = ("b", "c1", "r1", "c0")


def swap(piece, axes):
    return lax.all_to_all(piece, axes, split_axis=0, concat_axis=0, tiled=True)


def meet(piece):
    return lax.ppermute(piece, "core", [(0, 1), (1, 0)])


def shards(queries, keys, values, out_grad):
    core = lax.axis_index("core")
    r = 2 * lax.axis_index("r1") + core
    c = 2 * lax.axis_index("c1") + lax.axis_index("c0")
    at = jnp.stack([r, c, core]).astype(jnp.int32)
    wide = GROUP * D_HEAD
    grad_parts = call(split_grad, shape(HEADS, TOK // HEADS, wide), [], out_grad)
    grad_local = swap(grad_parts, "head").reshape(TOK, wide)
    data = swap(
        call(
            pack_body,
            shape(CHIPS, 3 * PART, 2 * D_HEAD),
            [pltpu.VMEM((GROUP, PART, 2 * D_HEAD), BF)],
            at, queries, keys, values, grad_local,
        ),
        CHIP_AXES,
    )
    other = meet(call(give_body, shape(CHIPS, 2 * PART, 2 * D_HEAD), [], data))
    stat = shape(GROUP, 2 * GROUP, SIDE, dtype=F32)
    tiles = [
        shape(FULL, SIDE, SIDE, dtype=F32),
        shape(GROUP, HALF, SIDE, dtype=F32),
        shape(GROUP, HALF, HALF, dtype=F32),
    ]
    stats, *saved = call(stats_body, [stat, *tiles, *tiles], [], at, data, other, micros=5)
    stats = swap(stats, ("c1", "c0"))
    half = PART // 2
    dkv, dq, give = call(
        grads_body,
        [
            shape(CHIPS, PART, 2 * D_HEAD),
            shape(CHIPS, half, 2 * D_HEAD),
            shape(CHIPS, PART + half, 2 * D_HEAD),
        ],
        [
            pltpu.VMEM(stat.shape[1:], F32),
            pltpu.VMEM((GROUP, SIDE, 2 * D_HEAD), BF),
            pltpu.VMEM((GROUP, SIDE, 2 * D_HEAD), BF),
            pltpu.VMEM((GROUP, D_HEAD, SIDE), F32),
            pltpu.VMEM((SIDE, 2 * D_HEAD), F32),
        ],
        data, other, stats, *saved,
        micros=7,
    )
    partial = call(
        pair_body, shape(CHIPS, 2 * PART, 2 * D_HEAD), [], at, dkv, dq, meet(give)
    )
    return tuple(call(sum_body, [shape(TOK, wide)] * 3, [], swap(partial, CHIP_AXES)))


def solution(mesh):
    ctx = (*CHIP_AXES, "core")
    split = Mesh(mesh.devices.reshape(4, 2, 2, 2, 2, HEADS), (*ctx, "head"))
    placed = (P(ctx, "head"), P(ctx, "head"), P(ctx, "head"), P((*ctx, "head"), None))
    return jax.shard_map(
        shards,
        mesh=split,
        in_specs=placed,
        out_specs=placed[:3],
        check_vma=False,
    )
```

time: 595 us -> 109 us (0.18)
  the two profiles are of different devices: /device:TPU:1 before, /device:TPU:8 now
where the time goes in v1:
time: 109 us
  blocking collectives  61.9 us (57%)
  starting transfers between devices  16.6 us (15%)
  waiting for transfers between devices  13.8 us (13%)
  Pallas kernels  12.5 us (11%)
  local copies, waits for them, and re-layouts  3.35 us (3%)
    all_to_all x3, blocking collectives, swap(): return lax.all_to_all(piece, axes, split_axis=0, concat_axis=0, tiled=True)  61.9 us
    all_to_all x1, starting transfers between devices, swap(): return lax.all_to_all(piece, axes, split_axis=0, concat_axis=0, tiled=True)  12.7 us
    pallas_call x7, Pallas kernels, call(): pl.pallas_call(body, out_shape=out_shapes, in_specs=[pl.BlockSpec(memory_...  12.5 us
    all_to_all x1, waiting for transfers between devices, swap(): return lax.all_to_all(piece, axes, split_axis=0, concat_axis=0, tiled=True)  10.2 us
    ppermute x2, starting transfers between devices, meet(): return lax.ppermute(piece, 'core', [(0, 1), (1, 0)])  3.84 us
    ppermute x2, waiting for transfers between devices, meet(): return lax.ppermute(piece, 'core', [(0, 1), (1, 0)])  3.56 us
    unnamed x8, local copies, waits for them, and re-layouts  3.35 us
  transfers between devices with their start and end apart: 3, of which 3 were waited for; matrix products, arithmetic and copies ran while one was open for 0% of the time, Pallas kernels for 0%

profile of v1, /device:TPU:8, one launch (start us, length us, event | category | flops | bytes accessed | tf_op | source)
XLA Modules:
  0.0 108.9 jit_solution(13559262991441554307)
XLA Ops:
  0.6 0.0 copy-start
  0.6 0.8 copy-done
  1.5 0.6 shard_map.67
  2.1 12.7 %all-to-all-start = ((bf16[8,16,256]{2,1,0:T(8,128)(2,1)}), bf16[8,16,256]{2,1,0:T(8,128)(2,1)S(1)}, u32[]{:S(2)}, u32[]{:S(2)}) async-start(bf16[8,16,256]{2,1,0:T(8,128)(2,1)} %shard_map.67), calls=%async_computation | async-start | bytes 131072 | tf_op jit(solution)/shard_map/all_to_all | solution.py:264
  14.8 0.1 pad_add_fusion.at
  14.9 10.2 %all-to-all-done = bf16[8,16,256]{2,1,0:T(8,128)(2,1)S(1)} async-done(((bf16[8,16,256]{2,1,0:T(8,128)(2,1)}), bf16[8,16,256]{2,1,0:T(8,128)(2,1)S(1)}, u32[]{:S(2)}, u32[]{:S(2)}) %all-to-all-start) | async-done | bytes 65568 | tf_op jit(solution)/shard_map/all_to_all | solution.py:264
  25.1 0.0 copy-start.1
  25.1 0.8 copy-done.1
  26.0 0.0 copy-start.2
  26.0 0.8 copy-done.2
  26.8 0.0 copy-start.3
  26.8 0.8 copy-done.3
  27.6 0.7 shard_map.68
  28.4 31.8 %all_to_all.20.data = bf16[32,96,128]{2,1,0:T(8,128)(2,1)S(1)} all-to-all(bf16[32,96,128]{2,1,0:T(8,128)(2,1)S(1)} %shard_map.68), channel_id=1, replica_groups=mesh['b'=4,'c1'=2,'r1'=2,'c0'=2,'core'=2,'head'=8] {'b','c1','r1','c0'}, dimensions={0} | all-to-all | bytes 1572864 | tf_op jit(solution)/shard_map/all_to_all | solution.py:264
  60.2 1.9 %collective-permute-start = (bf16[32,64,128]{2,1,0:T(8,128)(2,1)S(1)}, bf16[32,64,128]{2,1,0:T(8,128)(2,1)S(1)}, u32[]{:S(2)}, u32[]{:S(2)}) collective-permute-start(bf16[32,64,128]{2,1,0:T(8,128)(2,1)S(1)} %shard_map.69), channel_id=1, source_target_pairs={{0,8},{8,0},{1,9},{9,1},{2,10},{10,2},{3,11},{11,3},{4,12},{12,4},... | collective-permute-start | bytes 1572872 | tf_op jit(solution)/shard_map/ppermute | solution.py:268
  62.1 1.9 %collective-permute-done.other = bf16[32,64,128]{2,1,0:T(8,128)(2,1)S(1)} collective-permute-done((bf16[32,64,128]{2,1,0:T(8,128)(2,1)S(1)}, bf16[32,64,128]{2,1,0:T(8,128)(2,1)S(1)}, u32[]{:S(2)}, u32[]{:S(2)}) %collective-permute-start) | collective-permute-done | bytes 524320 | tf_op jit(solution)/shard_map/ppermute | solution.py:268
  64.0 5.4 %shard_map.70 = (f32[4,8,512]{2,1,0:T(8,128)S(1)}, f32[6,512,512]{2,1,0:T(8,128)S(1)}, f32[4,256,512]{2,1,0:T(8,128)S(1)}, f32[4,256,256]{2,1,0:T(8,128)S(1)}, f...) custom-call(s32[3]{0:T(128)S(1)} %pad_add_fusion.at, ...), custom_call_target="tpu_custom_call" | custom-call | flops 5000000000 | bytes 1048576 | tf_op jit(solution)/shard_map/pallas_call | solution.py:37
  69.4 7.0 %all_to_all.21.stats = f32[4,8,512]{2,1,0:T(8,128)S(1)} all-to-all(f32[4,8,512]{2,1,0:T(8,128)S(1)} %get-tuple-element.13), channel_id=1, replica_groups=mesh['b'=4,'c1'=2,'r1'=2,'c0'=2,'core'=2,'head'=8] {'c1','c0'}, dimensions={0} | all-to-all | bytes 131072 | tf_op jit(solution)/shard_map/all_to_all | solution.py:264
  76.5 4.2 %shard_map.71 = (bf16[32,32,128]{2,1,0:T(8,128)(2,1)S(1)}, bf16[32,16,128]{2,1,0:T(8,128)(2,1)S(1)}, bf16[32,48,128]{2,1,0:T(8,128)(2,1)S(1)}) custom-call(bf16[32,96,128]{2,1,0:T(8,128)(2,1)S(1)} %all_to_all.20.data, bf16[32,64,128]{2,1,0:T(8,128)(2,1)S(1)} %collective-permute-done.other, f32[4,8,512]{2,1,0:T(8,128)S(1)} %all_to_all.21.stats, ...), custom_call_target="tpu_custom_call" | custom-call | flops 7000000000 | bytes 1048576 | tf_op jit(solution)/shard_map/pallas_call | solution.py:37
  80.7 1.9 %collective-permute-start.1 = (bf16[32,48,128]{2,1,0:T(8,128)(2,1)S(1)}, bf16[32,48,128]{2,1,0:T(8,128)(2,1)S(1)}, u32[]{:S(2)}, u32[]{:S(2)}) collective-permute-start(bf16[32,48,128]{2,1,0:T(8,128)(2,1)S(1)} %get-tuple-element.22), channel_id=1, source_target_pairs={{0,8},{8,0},{1,9},{9,1},{2,10},{10,2},{3,11},{11,3},{4,12},{12,4},... | collective-permute-start | bytes 1179656 | tf_op jit(solution)/shard_map/ppermute | solution.py:268
  82.6 1.7 %collective-permute-done.1.got = bf16[32,48,128]{2,1,0:T(8,128)(2,1)S(1)} collective-permute-done((bf16[32,48,128]{2,1,0:T(8,128)(2,1)S(1)}, bf16[32,48,128]{2,1,0:T(8,128)(2,1)S(1)}, u32[]{:S(2)}, u32[]{:S(2)}) %collective-permute-start.1) | collective-permute-done | bytes 393248 | tf_op jit(solution)/shard_map/ppermute | solution.py:268
  84.3 0.6 shard_map.72
  84.9 23.1 %all_to_all.22.part = bf16[32,64,128]{2,1,0:T(8,128)(2,1)S(1)} all-to-all(bf16[32,64,128]{2,1,0:T(8,128)(2,1)S(1)} %shard_map.72), channel_id=1, replica_groups=mesh['b'=4,'c1'=2,'r1'=2,'c0'=2,'core'=2,'head'=8] {'b','c1','r1','c0'}, dimensions={0} | all-to-all | bytes 1048576 | tf_op jit(solution)/shard_map/all_to_all | solution.py:264
  108.1 0.8 shard_map.73
  (1 shorter events, 0.0 us)
Async XLA Ops:
  0.6 0.8 copy-start
  2.1 23.0 %all-to-all-start = ((bf16[8,16,256]{2,1,0:T(8,128)(2,1)}), bf16[8,16,256]{2,1,0:T(8,128)(2,1)S(1)}, u32[]{:S(2)}, u32[]{:S(2)}) async-start(bf16[8,16,256]{2,1,0:T(8,128)(2,1)} %shard_map.67), calls=%async_computation | async-start | bytes 131072 | tf_op jit(solution)/shard_map/all_to_all | solution.py:264
  25.1 0.8 copy-start.1
  26.0 0.8 copy-start.2
  26.8 0.8 copy-start.3
  60.2 3.8 %collective-permute-start = (bf16[32,64,128]{2,1,0:T(8,128)(2,1)S(1)}, bf16[32,64,128]{2,1,0:T(8,128)(2,1)S(1)}, u32[]{:S(2)}, u32[]{:S(2)}) collective-permute-start(bf16[32,64,128]{2,1,0:T(8,128)(2,1)S(1)} %shard_map.69), channel_id=1, source_target_pairs={{0,8},{8,0},{1,9},{9,1},{2,10},{10,2},{3,11},{11,3},{4,12},{12,4},... | collective-permute-start | bytes 1572872 | tf_op jit(solution)/shard_map/ppermute | solution.py:268
  80.7 3.6 %collective-permute-start.1 = (bf16[32,48,128]{2,1,0:T(8,128)(2,1)S(1)}, bf16[32,48,128]{2,1,0:T(8,128)(2,1)S(1)}, u32[]{:S(2)}, u32[]{:S(2)}) collective-permute-start(bf16[32,48,128]{2,1,0:T(8,128)(2,1)S(1)} %get-tuple-element.22), channel_id=1, source_target_pairs={{0,8},{8,0},{1,9},{9,1},{2,10},{10,2},{3,11},{11,3},{4,12},{12,4},... | collective-permute-start | bytes 1179656 | tf_op jit(solution)/shard_map/ppermute | solution.py:268

commit v2 on v1

--- a/solution.py
+++ b/solution.py
@@ -56,12 +56,12 @@
         out_ref[g] = grad[:, g * GROUP * D_HEAD : (g + 1) * GROUP * D_HEAD]
 
 
-def pack_body(at, q_ref, k_ref, v_ref, g_ref, out_ref, stage):
+def pack_body(at, q_ref, k_ref, v_ref, out_ref, stage):
     core = at[2]
     for b in range(GROUP):
         lanes = slice(b * D_HEAD, (b + 1) * D_HEAD)
         both = jnp.concatenate([k_ref[:, lanes], v_ref[:, lanes]], axis=1)
-        rows = jnp.concatenate([q_ref[:, lanes], g_ref[:, lanes]], axis=1)
+        rows = jnp.concatenate([q_ref[:, lanes], q_ref[:, lanes]], axis=1)
         stage[...] = rows.reshape(GROUP, PART, 2 * D_HEAD)
         for r1 in range(2):
             keep, give = stage[2 * r1 + core], stage[2 * r1 + 1 - core]
@@ -70,6 +70,22 @@
                 out_ref[to, :PART, :] = keep
                 out_ref[to, PART : 2 * PART, :] = both[c * PART : (c + 1) * PART, :]
                 out_ref[to, 2 * PART :, :] = give
+
+
+def add_grad(at, g_ref, part_ref, out_ref, stage):
+    core = at[2]
+    first = lax.broadcasted_iota(jnp.int32, (PART, 2 * D_HEAD), 1) < D_HEAD
+    for b in range(GROUP):
+        lanes = slice(b * D_HEAD, (b + 1) * D_HEAD)
+        rows = jnp.concatenate([g_ref[:, lanes], g_ref[:, lanes]], axis=1)
+        stage[...] = rows.reshape(GROUP, PART, 2 * D_HEAD)
+        for r1 in range(2):
+            keep, give = stage[2 * r1 + core], stage[2 * r1 + 1 - core]
+            for c in range(GROUP):
+                to = chip_of(b, r1, c)
+                out_ref[to, :PART, :] = jnp.where(first, part_ref[to, :PART, :], keep)
+                out_ref[to, PART : 2 * PART, :] = part_ref[to, PART : 2 * PART, :]
+                out_ref[to, 2 * PART :, :] = jnp.where(first, part_ref[to, 2 * PART :, :], give)
 
 
 def give_body(data, give_ref):
@@ -276,15 +292,10 @@
     wide = GROUP * D_HEAD
     grad_parts = call(split_grad, shape(HEADS, TOK // HEADS, wide), [], out_grad)
     grad_local = swap(grad_parts, "head").reshape(TOK, wide)
-    data = swap(
-        call(
-            pack_body,
-            shape(CHIPS, 3 * PART, 2 * D_HEAD),
-            [pltpu.VMEM((GROUP, PART, 2 * D_HEAD), BF)],
-            at, queries, keys, values, grad_local,
-        ),
-        CHIP_AXES,
-    )
+    message = shape(CHIPS, 3 * PART, 2 * D_HEAD)
+    stage = [pltpu.VMEM((GROUP, PART, 2 * D_HEAD), BF)]
+    part = call(pack_body, message, stage, at, queries, keys, values)
+    data = swap(call(add_grad, message, stage, at, grad_local, part), CHIP_AXES)
     other = meet(call(give_body, shape(CHIPS, 2 * PART, 2 * D_HEAD), [], data))
     stat = shape(GROUP, 2 * GROUP, SIDE, dtype=F32)
     tiles = [

time: 109 us -> 107 us (0.982)
  waiting for transfers between devices: 13.8 us -> 10.5 us
    all_to_all x1, waiting for transfers between devices: 10.2 us -> 6.93 us  [swap(): return lax.all_to_all(piece, axes, split_axis=0, concat_axis=0, tiled=True)]
    pallas_call x7 -> x8, Pallas kernels: 12.5 us -> 13.2 us  [call(): pl.pallas_call(body, out_shape=out_shapes, in_specs=[pl.BlockSpec(memory_...]
  transfers between devices with their start and end apart: 3 -> 3, of which waited for: 3 -> 3; matrix products, arithmetic and copies ran while one was open for 0% -> 0% of each run, Pallas kernels for 0% -> 1%
where the time goes in v2:
time: 107 us; the launch traced here: 106 us
  blocking collectives  61.9 us (58%)
  starting transfers between devices  16.6 us (16%)
  Pallas kernels  13.2 us (12%)
  waiting for transfers between devices  10.5 us (10%)
  local copies, waits for them, and re-layouts  3.35 us (3%)
    all_to_all x3, blocking collectives, swap(): return lax.all_to_all(piece, axes, split_axis=0, concat_axis=0, tiled=True)  61.9 us
    pallas_call x8, Pallas kernels, call(): pl.pallas_call(body, out_shape=out_shapes, in_specs=[pl.BlockSpec(memory_...  13.2 us
    all_to_all x1, starting transfers between devices, swap(): return lax.all_to_all(piece, axes, split_axis=0, concat_axis=0, tiled=True)  12.7 us
    all_to_all x1, waiting for transfers between devices, swap(): return lax.all_to_all(piece, axes, split_axis=0, concat_axis=0, tiled=True)  6.93 us
    ppermute x2, starting transfers between devices, meet(): return lax.ppermute(piece, 'core', [(0, 1), (1, 0)])  3.84 us
    ppermute x2, waiting for transfers between devices, meet(): return lax.ppermute(piece, 'core', [(0, 1), (1, 0)])  3.56 us
    unnamed x8, local copies, waits for them, and re-layouts  3.35 us
  transfers between devices with their start and end apart: 3, of which 3 were waited for; matrix products, arithmetic and copies ran while one was open for 0% of the time, Pallas kernels for 1%

profile of v2, /device:TPU:8, one launch (start us, length us, event | category | flops | bytes accessed | tf_op | source)
XLA Modules:
  0.0 106.4 jit_solution(7863891328104001032)
XLA Ops:
  0.6 0.0 copy-start
  0.6 0.8 copy-done
  1.5 0.6 shard_map.67
  2.1 12.7 %all-to-all-start = ((bf16[8,16,256]{2,1,0:T(8,128)(2,1)}), bf16[8,16,256]{2,1,0:T(8,128)(2,1)S(1)}, u32[]{:S(2)}, u32[]{:S(2)}) async-start(bf16[8,16,256]{2,1,0:T(8,128)(2,1)} %shard_map.67), calls=%async_computation | async-start | bytes 131072 | tf_op jit(solution)/shard_map/all_to_all | solution.py:280
  14.8 0.1 pad_add_fusion.at
  14.9 0.0 copy-start.1
  14.9 0.8 copy-done.1
  15.8 0.0 copy-start.2
  15.8 0.8 copy-done.2
  16.6 0.0 copy-start.3
  16.6 0.8 copy-done.3
  17.4 0.7 shard_map.68.part_ref
  18.2 6.9 %all-to-all-done = bf16[8,16,256]{2,1,0:T(8,128)(2,1)S(1)} async-done(((bf16[8,16,256]{2,1,0:T(8,128)(2,1)}), bf16[8,16,256]{2,1,0:T(8,128)(2,1)S(1)}, u32[]{:S(2)}, u32[]{:S(2)}) %all-to-all-start) | async-done | bytes 65568 | tf_op jit(solution)/shard_map/all_to_all | solution.py:280
  25.1 0.7 shard_map.69
  25.8 31.8 %all_to_all.20.data = bf16[32,96,128]{2,1,0:T(8,128)(2,1)S(1)} all-to-all(bf16[32,96,128]{2,1,0:T(8,128)(2,1)S(1)} %shard_map.69), channel_id=1, replica_groups=mesh['b'=4,'c1'=2,'r1'=2,'c0'=2,'core'=2,'head'=8] {'b','c1','r1','c0'}, dimensions={0} | all-to-all | bytes 1572864 | tf_op jit(solution)/shard_map/all_to_all | solution.py:280
  57.6 1.9 %collective-permute-start = (bf16[32,64,128]{2,1,0:T(8,128)(2,1)S(1)}, bf16[32,64,128]{2,1,0:T(8,128)(2,1)S(1)}, u32[]{:S(2)}, u32[]{:S(2)}) collective-permute-start(bf16[32,64,128]{2,1,0:T(8,128)(2,1)S(1)} %shard_map.70), channel_id=1, source_target_pairs={{0,8},{8,0},{1,9},{9,1},{2,10},{10,2},{3,11},{11,3},{4,12},{12,4},... | collective-permute-start | bytes 1572872 | tf_op jit(solution)/shard_map/ppermute | solution.py:284
  59.6 1.9 %collective-permute-done.other = bf16[32,64,128]{2,1,0:T(8,128)(2,1)S(1)} collective-permute-done((bf16[32,64,128]{2,1,0:T(8,128)(2,1)S(1)}, bf16[32,64,128]{2,1,0:T(8,128)(2,1)S(1)}, u32[]{:S(2)}, u32[]{:S(2)}) %collective-permute-start) | collective-permute-done | bytes 524320 | tf_op jit(solution)/shard_map/ppermute | solution.py:284
  61.4 5.4 %shard_map.71 = (f32[4,8,512]{2,1,0:T(8,128)S(1)}, f32[6,512,512]{2,1,0:T(8,128)S(1)}, f32[4,256,512]{2,1,0:T(8,128)S(1)}, f32[4,256,256]{2,1,0:T(8,128)S(1)}, f...) custom-call(s32[3]{0:T(128)S(1)} %pad_add_fusion.at, ...), custom_call_target="tpu_custom_call" | custom-call | flops 5000000000 | bytes 1048576 | tf_op jit(solution)/shard_map/pallas_call | solution.py:37
  66.9 7.1 %all_to_all.21.stats = f32[4,8,512]{2,1,0:T(8,128)S(1)} all-to-all(f32[4,8,512]{2,1,0:T(8,128)S(1)} %get-tuple-element.13), channel_id=1, replica_groups=mesh['b'=4,'c1'=2,'r1'=2,'c0'=2,'core'=2,'head'=8] {'c1','c0'}, dimensions={0} | all-to-all | bytes 131072 | tf_op jit(solution)/shard_map/all_to_all | solution.py:280
  73.9 4.2 %shard_map.72 = (bf16[32,32,128]{2,1,0:T(8,128)(2,1)S(1)}, bf16[32,16,128]{2,1,0:T(8,128)(2,1)S(1)}, bf16[32,48,128]{2,1,0:T(8,128)(2,1)S(1)}) custom-call(bf16[32,96,128]{2,1,0:T(8,128)(2,1)S(1)} %all_to_all.20.data, bf16[32,64,128]{2,1,0:T(8,128)(2,1)S(1)} %collective-permute-done.other, f32[4,8,512]{2,1,0:T(8,128)S(1)} %all_to_all.21.stats, ...), custom_call_target="tpu_custom_call" | custom-call | flops 7000000000 | bytes 1048576 | tf_op jit(solution)/shard_map/pallas_call | solution.py:37
  78.2 1.9 %collective-permute-start.1 = (bf16[32,48,128]{2,1,0:T(8,128)(2,1)S(1)}, bf16[32,48,128]{2,1,0:T(8,128)(2,1)S(1)}, u32[]{:S(2)}, u32[]{:S(2)}) collective-permute-start(bf16[32,48,128]{2,1,0:T(8,128)(2,1)S(1)} %get-tuple-element.22), channel_id=1, source_target_pairs={{0,8},{8,0},{1,9},{9,1},{2,10},{10,2},{3,11},{11,3},{4,12},{12,4},... | collective-permute-start | bytes 1179656 | tf_op jit(solution)/shard_map/ppermute | solution.py:284
  80.1 1.7 %collective-permute-done.1.got = bf16[32,48,128]{2,1,0:T(8,128)(2,1)S(1)} collective-permute-done((bf16[32,48,128]{2,1,0:T(8,128)(2,1)S(1)}, bf16[32,48,128]{2,1,0:T(8,128)(2,1)S(1)}, u32[]{:S(2)}, u32[]{:S(2)}) %collective-permute-start.1) | collective-permute-done | bytes 393248 | tf_op jit(solution)/shard_map/ppermute | solution.py:284
  81.8 0.6 shard_map.73
  82.4 23.1 %all_to_all.22.part = bf16[32,64,128]{2,1,0:T(8,128)(2,1)S(1)} all-to-all(bf16[32,64,128]{2,1,0:T(8,128)(2,1)S(1)} %shard_map.73), channel_id=1, replica_groups=mesh['b'=4,'c1'=2,'r1'=2,'c0'=2,'core'=2,'head'=8] {'b','c1','r1','c0'}, dimensions={0} | all-to-all | bytes 1048576 | tf_op jit(solution)/shard_map/all_to_all | solution.py:280
  105.5 0.8 shard_map.74
  (1 shorter events, 0.0 us)
Async XLA Ops:
  0.6 0.8 copy-start
  2.1 23.0 %all-to-all-start = ((bf16[8,16,256]{2,1,0:T(8,128)(2,1)}), bf16[8,16,256]{2,1,0:T(8,128)(2,1)S(1)}, u32[]{:S(2)}, u32[]{:S(2)}) async-start(bf16[8,16,256]{2,1,0:T(8,128)(2,1)} %shard_map.67), calls=%async_computation | async-start | bytes 131072 | tf_op jit(solution)/shard_map/all_to_all | solution.py:280
  14.9 0.8 copy-start.1
  15.8 0.8 copy-start.2
  16.6 0.8 copy-start.3
  57.6 3.8 %collective-permute-start = (bf16[32,64,128]{2,1,0:T(8,128)(2,1)S(1)}, bf16[32,64,128]{2,1,0:T(8,128)(2,1)S(1)}, u32[]{:S(2)}, u32[]{:S(2)}) collective-permute-start(bf16[32,64,128]{2,1,0:T(8,128)(2,1)S(1)} %shard_map.70), channel_id=1, source_target_pairs={{0,8},{8,0},{1,9},{9,1},{2,10},{10,2},{3,11},{11,3},{4,12},{12,4},... | collective-permute-start | bytes 1572872 | tf_op jit(solution)/shard_map/ppermute | solution.py:284
  78.2 3.6 %collective-permute-start.1 = (bf16[32,48,128]{2,1,0:T(8,128)(2,1)S(1)}, bf16[32,48,128]{2,1,0:T(8,128)(2,1)S(1)}, u32[]{:S(2)}, u32[]{:S(2)}) collective-permute-start(bf16[32,48,128]{2,1,0:T(8,128)(2,1)S(1)} %get-tuple-element.22), channel_id=1, source_target_pairs={{0,8},{8,0},{1,9},{9,1},{2,10},{10,2},{3,11},{11,3},{4,12},{12,4},... | collective-permute-start | bytes 1179656 | tf_op jit(solution)/shard_map/ppermute | solution.py:284

commit v3 on v1

--- a/solution.py
+++ b/solution.py
@@ -51,24 +51,50 @@
     return jax.ShapeDtypeStruct(dims, dtype)
 
 
-def split_grad(grad, out_ref):
-    for g in range(HEADS):
-        out_ref[g] = grad[:, g * GROUP * D_HEAD : (g + 1) * GROUP * D_HEAD]
-
-
-def pack_body(at, q_ref, k_ref, v_ref, g_ref, out_ref, stage):
-    core = at[2]
+def split_grad(at, grad, keep_ref, give_ref):
+    half = GROUP * GROUP * D_HEAD
+    for out, side in ((keep_ref, at[3]), (give_ref, 1 - at[3])):
+        out[...] = grad[:, pl.ds(pl.multiple_of(side * half, half), half)]
+
+
+def regroup_grad(keep, got, out_ref):
+    wide, few = GROUP * D_HEAD, TOK // HEADS
+    for x in range(GROUP):
+        out_ref[x, :few, :] = keep[:, x * wide : (x + 1) * wide]
+        out_ref[x, few:, :] = got[:, x * wide : (x + 1) * wide]
+
+
+def pack_body(q_hbm, k_hbm, v_hbm, out_ref, q_ref, k_ref, v_ref, sems):
+    pairs = ((q_hbm, q_ref), (k_hbm, k_ref), (v_hbm, v_ref))
+    copies = [pltpu.make_async_copy(*pair, sems.at[i]) for i, pair in enumerate(pairs)]
+    for copy in copies:
+        copy.start()
+    for copy in copies:
+        copy.wait()
     for b in range(GROUP):
         lanes = slice(b * D_HEAD, (b + 1) * D_HEAD)
-        both = jnp.concatenate([k_ref[:, lanes], v_ref[:, lanes]], axis=1)
-        rows = jnp.concatenate([q_ref[:, lanes], g_ref[:, lanes]], axis=1)
-        stage[...] = rows.reshape(GROUP, PART, 2 * D_HEAD)
+        for i, halves_of in enumerate(((q_ref, q_ref), (k_ref, v_ref))):
+            out_ref[i, b] = jnp.concatenate([ref[:, lanes] for ref in halves_of], axis=1)
+
+
+def add_grad(at, g_ref, part_ref, out_ref, stage):
+    core, few = at[2], TOK // HEADS
+    first = lax.broadcasted_iota(jnp.int32, (few, 2 * D_HEAD), 1) < D_HEAD
+    for b in range(GROUP):
+        lanes = slice(b * D_HEAD, (b + 1) * D_HEAD)
+        for x in range(GROUP):
+            for side in range(2):
+                block = g_ref[x, side * few : (side + 1) * few, lanes]
+                block = jnp.concatenate([block, block], axis=1)
+                r, line = 2 * (at[3] ^ side) + x // 2, (x % 2) * few
+                tokens = pl.ds(pl.multiple_of(r * PART + line, few), few)
+                stage[r, line : line + few, :] = jnp.where(first, part_ref[0, b, tokens, :], block)
         for r1 in range(2):
             keep, give = stage[2 * r1 + core], stage[2 * r1 + 1 - core]
             for c in range(GROUP):
                 to = chip_of(b, r1, c)
                 out_ref[to, :PART, :] = keep
-                out_ref[to, PART : 2 * PART, :] = both[c * PART : (c + 1) * PART, :]
+                out_ref[to, PART : 2 * PART, :] = part_ref[1, b, c * PART : (c + 1) * PART, :]
                 out_ref[to, 2 * PART :, :] = give
 
 
@@ -264,28 +290,33 @@
     return lax.all_to_all(piece, axes, split_axis=0, concat_axis=0, tiled=True)
 
 
-def meet(piece):
-    return lax.ppermute(piece, "core", [(0, 1), (1, 0)])
+def meet(piece, axis):
+    return lax.ppermute(piece, axis, [(0, 1), (1, 0)])
 
 
 def shards(queries, keys, values, out_grad):
     core = lax.axis_index("core")
     r = 2 * lax.axis_index("r1") + core
     c = 2 * lax.axis_index("c1") + lax.axis_index("c0")
-    at = jnp.stack([r, c, core]).astype(jnp.int32)
+    at = jnp.stack([r, c, core, lax.axis_index("zhi")]).astype(jnp.int32)
     wide = GROUP * D_HEAD
-    grad_parts = call(split_grad, shape(HEADS, TOK // HEADS, wide), [], out_grad)
-    grad_local = swap(grad_parts, "head").reshape(TOK, wide)
-    data = swap(
-        call(
-            pack_body,
-            shape(CHIPS, 3 * PART, 2 * D_HEAD),
-            [pltpu.VMEM((GROUP, PART, 2 * D_HEAD), BF)],
-            at, queries, keys, values, grad_local,
-        ),
-        CHIP_AXES,
-    )
-    other = meet(call(give_body, shape(CHIPS, 2 * PART, 2 * D_HEAD), [], data))
+    few = TOK // HEADS
+    keep, give = call(split_grad, [shape(few, GROUP * wide)] * 2, [], at, out_grad)
+    regrouped = call(regroup_grad, shape(GROUP, 2 * few, wide), [], keep, meet(give, "zhi"))
+    grad_local = swap(regrouped, "x")
+    message = shape(CHIPS, 3 * PART, 2 * D_HEAD)
+    local = [pltpu.VMEM((TOK, wide), BF)] * 3
+    part = call(
+        pack_body,
+        shape(2, GROUP, TOK, 2 * D_HEAD),
+        [*local, pltpu.SemaphoreType.DMA((3,))],
+        queries, keys, values,
+        space=pl.ANY,
+        vmem=60,
+    )
+    stage = pltpu.VMEM((GROUP, PART, 2 * D_HEAD), BF)
+    data = swap(call(add_grad, message, [stage], at, grad_local, part), CHIP_AXES)
+    other = meet(call(give_body, shape(CHIPS, 2 * PART, 2 * D_HEAD), [], data), "core")
     stat = shape(GROUP, 2 * GROUP, SIDE, dtype=F32)
     tiles = [
         shape(FULL, SIDE, SIDE, dtype=F32),
@@ -313,15 +344,16 @@
         micros=7,
     )
     partial = call(
-        pair_body, shape(CHIPS, 2 * PART, 2 * D_HEAD), [], at, dkv, dq, meet(give)
+        pair_body, shape(CHIPS, 2 * PART, 2 * D_HEAD), [], at, dkv, dq, meet(give, "core")
     )
     return tuple(call(sum_body, [shape(TOK, wide)] * 3, [], swap(partial, CHIP_AXES)))
 
 
 def solution(mesh):
     ctx = (*CHIP_AXES, "core")
-    split = Mesh(mesh.devices.reshape(4, 2, 2, 2, 2, HEADS), (*ctx, "head"))
-    placed = (P(ctx, "head"), P(ctx, "head"), P(ctx, "head"), P((*ctx, "head"), None))
+    heads = ("zhi", "x")
+    split = Mesh(mesh.devices.reshape(4, 2, 2, 2, 2, 2, 4), (*ctx, *heads))
+    placed = (P(ctx, heads), P(ctx, heads), P(ctx, heads), P((*ctx, *heads), None))
     return jax.shard_map(
         shards,
         mesh=split,

time: 109 us -> 107 us (0.982)
  waiting for transfers between devices: 13.8 us -> 9.33 us
  starting transfers between devices: 16.6 us -> 19 us
  Pallas kernels: 12.5 us -> 14.8 us
  local copies, waits for them, and re-layouts: 3.35 us -> 1.79 us
    ppermute x2 -> x3, starting transfers between devices: 3.84 us -> 14.8 us  [meet(): return lax.ppermute(piece, axis, [(0, 1), (1, 0)])]
    all_to_all x1, starting transfers between devices: 12.7 us -> 4.29 us  [swap(): return lax.all_to_all(piece, axes, split_axis=0, concat_axis=0, tiled=True)]
    all_to_all x1, waiting for transfers between devices: 10.2 us -> 3.86 us  [swap(): return lax.all_to_all(piece, axes, split_axis=0, concat_axis=0, tiled=True)]
    pallas_call x7 -> x9, Pallas kernels: 12.5 us -> 14.8 us  [call(): pl.pallas_call(body, out_shape=out_shapes, in_specs=[pl.BlockSpec(memory_...]
    ppermute x2 -> x3, waiting for transfers between devices: 3.56 us -> 5.48 us  [meet(): return lax.ppermute(piece, axis, [(0, 1), (1, 0)])]
    unnamed x8 -> x4, local copies, waits for them, and re-layouts: 3.35 us -> 1.79 us
  transfers between devices with their start and end apart: 3 -> 4, of which waited for: 3 -> 4; matrix products, arithmetic and copies ran while one was open for 0% -> 0% of each run, Pallas kernels for 0% -> 2%
where the time goes in v3:
time: 107 us
  blocking collectives  61 us (57%)
  starting transfers between devices  19 us (18%)
  Pallas kernels  14.8 us (14%)
  waiting for transfers between devices  9.33 us (9%)
  local copies, waits for them, and re-layouts  1.79 us (2%)
    all_to_all x3, blocking collectives, swap(): return lax.all_to_all(piece, axes, split_axis=0, concat_axis=0, tiled=True)  61 us
    pallas_call x9, Pallas kernels, call(): pl.pallas_call(body, out_shape=out_shapes, in_specs=[pl.BlockSpec(memory_...  14.8 us
    ppermute x3, starting transfers between devices, meet(): return lax.ppermute(piece, axis, [(0, 1), (1, 0)])  14.8 us
    ppermute x3, waiting for transfers between devices, meet(): return lax.ppermute(piece, axis, [(0, 1), (1, 0)])  5.48 us
    all_to_all x1, starting transfers between devices, swap(): return lax.all_to_all(piece, axes, split_axis=0, concat_axis=0, tiled=True)  4.29 us
    all_to_all x1, waiting for transfers between devices, swap(): return lax.all_to_all(piece, axes, split_axis=0, concat_axis=0, tiled=True)  3.86 us
  transfers between devices with their start and end apart: 4, of which 4 were waited for; matrix products, arithmetic and copies ran while one was open for 0% of the time, Pallas kernels for 2%

profile of v3, /device:TPU:8, one launch (start us, length us, event | category | flops | bytes accessed | tf_op | source)
XLA Modules:
  0.0 106.8 jit_solution(7088860051477911975)
XLA Ops:
  0.6 0.1 pad_add_fusion.at
  0.7 0.0 copy-start
  0.7 0.8 copy-done
  1.6 0.5 shard_map.67
  2.1 10.9 %collective-permute-start = (bf16[16,1024]{1,0:T(8,128)(2,1)S(1)}, bf16[16,1024]{1,0:T(8,128)(2,1)S(1)}, u32[]{:S(2)}, u32[]{:S(2)}) collective-permute-start(bf16[16,1024]{1,0:T(8,128)(2,1)S(1)} %get-tuple-element.16), channel_id=1, source_target_pairs={{0,4},{4,0},{1,5},{5,1},{2,6},{6,2},{3,7},{7,3},{8,12},{12,8},{9,1... | collective-permute-start | bytes 98312 | tf_op jit(solution)/shard_map/ppermute | solution.py:294
  13.0 1.9 %collective-permute-done.got = bf16[16,1024]{1,0:T(8,128)(2,1)S(1)} collective-permute-done((bf16[16,1024]{1,0:T(8,128)(2,1)S(1)}, bf16[16,1024]{1,0:T(8,128)(2,1)S(1)}, u32[]{:S(2)}, u32[]{:S(2)}) %collective-permute-start) | collective-permute-done | bytes 32800 | tf_op jit(solution)/shard_map/ppermute | solution.py:294
  15.0 0.6 shard_map.68
  15.6 4.3 %all-to-all-start = ((bf16[4,32,256]{2,1,0:T(8,128)(2,1)}), bf16[4,32,256]{2,1,0:T(8,128)(2,1)S(1)}, u32[]{:S(2)}, u32[]{:S(2)}) async-start(bf16[4,32,256]{2,1,0:T(8,128)(2,1)} %shard_map.68), calls=%async_computation | async-start | bytes 131072 | tf_op jit(solution)/shard_map/all_to_all | solution.py:290
  19.9 1.8 %shard_map.69.part_ref = bf16[2,4,128,128]{3,2,1,0:T(8,128)(2,1)} custom-call(bf16[128,256]{1,0:T(8,128)(2,1)} %q_hbm.1, bf16[128,256]{1,0:T(8,128)(2,1)} %k_hbm.1, bf16[128,256]{1,0:T(8,128)(2,1)} %v_hbm.1), custom_call_target="tpu_custom_call" | custom-call | flops 1000000000 | bytes 1048576 | tf_op jit(solution)/shard_map/pallas_call | solution.py:37
  21.6 3.9 %all-to-all-done.g_ref = bf16[4,32,256]{2,1,0:T(8,128)(2,1)S(1)} async-done(((bf16[4,32,256]{2,1,0:T(8,128)(2,1)}), bf16[4,32,256]{2,1,0:T(8,128)(2,1)S(1)}, u32[]{:S(2)}, u32[]{:S(2)}) %all-to-all-start) | async-done | bytes 65568 | tf_op jit(solution)/shard_map/all_to_all | solution.py:290
  25.5 0.0 copy-start.1
  25.5 0.9 copy-done.1
  26.5 0.7 shard_map.70
  27.2 30.9 %all_to_all.20.data = bf16[32,96,128]{2,1,0:T(8,128)(2,1)S(1)} all-to-all(bf16[32,96,128]{2,1,0:T(8,128)(2,1)S(1)} %shard_map.70), channel_id=1, replica_groups=mesh['b'=4,'c1'=2,'r1'=2,'c0'=2,'core'=2,'zhi'=2,'x'=4] {'b','c1','r1','..., dimensions={0} | all-to-all | bytes 1572864 | tf_op jit(solution)/shard_map/all_to_all | solution.py:290
  58.1 1.9 %collective-permute-start.1 = (bf16[32,64,128]{2,1,0:T(8,128)(2,1)S(1)}, bf16[32,64,128]{2,1,0:T(8,128)(2,1)S(1)}, u32[]{:S(2)}, u32[]{:S(2)}) collective-permute-start(bf16[32,64,128]{2,1,0:T(8,128)(2,1)S(1)} %shard_map.71), channel_id=1, source_target_pairs={{0,8},{8,0},{1,9},{9,1},{2,10},{10,2},{3,11},{11,3},{4,12},{12,4},... | collective-permute-start | bytes 1572872 | tf_op jit(solution)/shard_map/ppermute | solution.py:294
  60.0 1.9 %collective-permute-done.1.other = bf16[32,64,128]{2,1,0:T(8,128)(2,1)S(1)} collective-permute-done((bf16[32,64,128]{2,1,0:T(8,128)(2,1)S(1)}, bf16[32,64,128]{2,1,0:T(8,128)(2,1)S(1)}, u32[]{:S(2)}, u32[]{:S(2)}) %collective-permute-start.1) | collective-permute-done | bytes 524320 | tf_op jit(solution)/shard_map/ppermute | solution.py:294
  61.9 5.4 %shard_map.72 = (f32[4,8,512]{2,1,0:T(8,128)S(1)}, f32[6,512,512]{2,1,0:T(8,128)S(1)}, f32[4,256,512]{2,1,0:T(8,128)S(1)}, f32[4,256,256]{2,1,0:T(8,128)S(1)}, f...) custom-call(s32[4]{0:T(128)S(1)} %pad_add_fusion.at, ...), custom_call_target="tpu_custom_call" | custom-call | flops 5000000000 | bytes 1048576 | tf_op jit(solution)/shard_map/pallas_call | solution.py:37
  67.3 6.9 %all_to_all.21.stats = f32[4,8,512]{2,1,0:T(8,128)S(1)} all-to-all(f32[4,8,512]{2,1,0:T(8,128)S(1)} %get-tuple-element.17), channel_id=1, replica_groups=mesh['b'=4,'c1'=2,'r1'=2,'c0'=2,'core'=2,'zhi'=2,'x'=4] {'c1','c0'}, dimensions={0} | all-to-all | bytes 131072 | tf_op jit(solution)/shard_map/all_to_all | solution.py:290
  74.2 4.2 %shard_map.73 = (bf16[32,32,128]{2,1,0:T(8,128)(2,1)S(1)}, bf16[32,16,128]{2,1,0:T(8,128)(2,1)S(1)}, bf16[32,48,128]{2,1,0:T(8,128)(2,1)S(1)}) custom-call(bf16[32,96,128]{2,1,0:T(8,128)(2,1)S(1)} %all_to_all.20.data, bf16[32,64,128]{2,1,0:T(8,128)(2,1)S(1)} %collective-permute-done.1.other, f32[4,8,512]{2,1,0:T(8,128)S(1)} %all_to_all.21.stats, ...), custom_call_target="tpu_custom_call" | custom-call | flops 7000000000 | bytes 1048576 | tf_op jit(solution)/shard_map/pallas_call | solution.py:37
  78.5 1.9 %collective-permute-start.2 = (bf16[32,48,128]{2,1,0:T(8,128)(2,1)S(1)}, bf16[32,48,128]{2,1,0:T(8,128)(2,1)S(1)}, u32[]{:S(2)}, u32[]{:S(2)}) collective-permute-start(bf16[32,48,128]{2,1,0:T(8,128)(2,1)S(1)} %get-tuple-element.26), channel_id=1, source_target_pairs={{0,8},{8,0},{1,9},{9,1},{2,10},{10,2},{3,11},{11,3},{4,12},{12,4},... | collective-permute-start | bytes 1179656 | tf_op jit(solution)/shard_map/ppermute | solution.py:294
  80.4 1.7 %collective-permute-done.2.got = bf16[32,48,128]{2,1,0:T(8,128)(2,1)S(1)} collective-permute-done((bf16[32,48,128]{2,1,0:T(8,128)(2,1)S(1)}, bf16[32,48,128]{2,1,0:T(8,128)(2,1)S(1)}, u32[]{:S(2)}, u32[]{:S(2)}) %collective-permute-start.2) | collective-permute-done | bytes 393248 | tf_op jit(solution)/shard_map/ppermute | solution.py:294
  82.1 0.6 shard_map.74
  82.7 23.3 %all_to_all.22.part = bf16[32,64,128]{2,1,0:T(8,128)(2,1)S(1)} all-to-all(bf16[32,64,128]{2,1,0:T(8,128)(2,1)S(1)} %shard_map.74), channel_id=1, replica_groups=mesh['b'=4,'c1'=2,'r1'=2,'c0'=2,'core'=2,'zhi'=2,'x'=4] {'b','c1','r1','..., dimensions={0} | all-to-all | bytes 1048576 | tf_op jit(solution)/shard_map/all_to_all | solution.py:290
  106.0 0.8 shard_map.75
  (1 shorter events, 0.0 us)
Async XLA Ops:
  0.7 0.8 copy-start
  2.1 12.8 %collective-permute-start = (bf16[16,1024]{1,0:T(8,128)(2,1)S(1)}, bf16[16,1024]{1,0:T(8,128)(2,1)S(1)}, u32[]{:S(2)}, u32[]{:S(2)}) collective-permute-start(bf16[16,1024]{1,0:T(8,128)(2,1)S(1)} %get-tuple-element.16), channel_id=1, source_target_pairs={{0,4},{4,0},{1,5},{5,1},{2,6},{6,2},{3,7},{7,3},{8,12},{12,8},{9,1... | collective-permute-start | bytes 98312 | tf_op jit(solution)/shard_map/ppermute | solution.py:294
  15.6 9.9 %all-to-all-start = ((bf16[4,32,256]{2,1,0:T(8,128)(2,1)}), bf16[4,32,256]{2,1,0:T(8,128)(2,1)S(1)}, u32[]{:S(2)}, u32[]{:S(2)}) async-start(bf16[4,32,256]{2,1,0:T(8,128)(2,1)} %shard_map.68), calls=%async_computation | async-start | bytes 131072 | tf_op jit(solution)/shard_map/all_to_all | solution.py:290
  25.5 1.0 copy-start.1
  58.1 3.8 %collective-permute-start.1 = (bf16[32,64,128]{2,1,0:T(8,128)(2,1)S(1)}, bf16[32,64,128]{2,1,0:T(8,128)(2,1)S(1)}, u32[]{:S(2)}, u32[]{:S(2)}) collective-permute-start(bf16[32,64,128]{2,1,0:T(8,128)(2,1)S(1)} %shard_map.71), channel_id=1, source_target_pairs={{0,8},{8,0},{1,9},{9,1},{2,10},{10,2},{3,11},{11,3},{4,12},{12,4},... | collective-permute-start | bytes 1572872 | tf_op jit(solution)/shard_map/ppermute | solution.py:294
  78.5 3.6 %collective-permute-start.2 = (bf16[32,48,128]{2,1,0:T(8,128)(2,1)S(1)}, bf16[32,48,128]{2,1,0:T(8,128)(2,1)S(1)}, u32[]{:S(2)}, u32[]{:S(2)}) collective-permute-start(bf16[32,48,128]{2,1,0:T(8,128)(2,1)S(1)} %get-tuple-element.26), channel_id=1, source_target_pairs={{0,8},{8,0},{1,9},{9,1},{2,10},{10,2},{3,11},{11,3},{4,12},{12,4},... | collective-permute-start | bytes 1179656 | tf_op jit(solution)/shard_map/ppermute | solution.py:294

commit v4 on v2

--- a/solution.py
+++ b/solution.py
@@ -29,7 +29,11 @@
 
 
 def chip_of(b, r1, c):
-    return b * 8 + (c // 2) * 4 + r1 * 2 + c % 2
+    return (r1 * 2 + c % 2) * 8 + b * 2 + c // 2
+
+
+def line_of(u, half):
+    return [z * 8 + 2 * u + half for z in range(QUAD)]
 
 
 def call(body, out_shapes, scratch, *operands, micros=1, space=pltpu.VMEM, vmem=24):
@@ -111,10 +115,10 @@
 def blocks(own, other, at):
     return jnp.concatenate(
         [
-            ref[at * PER + half * QUAD : at * PER + (half + 1) * QUAD, first : first + PART, :]
-            .reshape(HALF // 2, 2 * D_HEAD)
+            ref[chip, first : first + PART, :]
             for half in range(2)
             for ref, first in (own, other)
+            for chip in line_of(at, half)
         ],
         axis=0,
     )
@@ -233,16 +237,16 @@
             dkv_acc[...] += both_grads(p, ds, u, slice(0, SIDE))
         done = (dkv_acc[...] * factor).astype(BF).reshape(2, 2, QUAD, PART, 2 * D_HEAD)
         for half in range(2):
-            chips = slice(v * PER + half * QUAD, v * PER + (half + 1) * QUAD)
-            dkv_ref[chips] = done[half, 0]
-            give_ref[chips, :PART, :] = done[half, 1]
+            for i, chip in enumerate(line_of(v, half)):
+                dkv_ref[chip] = done[half, 0, i]
+                give_ref[chip, :PART, :] = done[half, 1, i]
     for u in range(GROUP):
         dq = (dq_acc[u] * SCALE).T.astype(BF).reshape(2, 2, QUAD, PART, D_HEAD)
         dq = jnp.concatenate([dq[..., : PART // 2, :], dq[..., PART // 2 :, :]], axis=4)
         for half in range(2):
-            chips = slice(u * PER + half * QUAD, u * PER + (half + 1) * QUAD)
-            dq_ref[chips] = dq[half, 0]
-            give_ref[chips, PART:, :] = dq[half, 1]
+            for i, chip in enumerate(line_of(u, half)):
+                dq_ref[chip] = dq[half, 0, i]
+                give_ref[chip, PART:, :] = dq[half, 1, i]
 
 
 def pair_body(at, dkv, dq, got, out_ref):
@@ -274,6 +278,7 @@
 
 
 CHIP_AXES = ("b", "c1", "r1", "c0")
+SWAP_AXES = ("r1", "c0", "b", "c1")
 
 
 def swap(piece, axes):
@@ -295,7 +300,7 @@
     message = shape(CHIPS, 3 * PART, 2 * D_HEAD)
     stage = [pltpu.VMEM((GROUP, PART, 2 * D_HEAD), BF)]
     part = call(pack_body, message, stage, at, queries, keys, values)
-    data = swap(call(add_grad, message, stage, at, grad_local, part), CHIP_AXES)
+    data = swap(call(add_grad, message, stage, at, grad_local, part), SWAP_AXES)
     other = meet(call(give_body, shape(CHIPS, 2 * PART, 2 * D_HEAD), [], data))
     stat = shape(GROUP, 2 * GROUP, SIDE, dtype=F32)
     tiles = [
@@ -326,7 +331,7 @@
     partial = call(
         pair_body, shape(CHIPS, 2 * PART, 2 * D_HEAD), [], at, dkv, dq, meet(give)
     )
-    return tuple(call(sum_body, [shape(TOK, wide)] * 3, [], swap(partial, CHIP_AXES)))
+    return tuple(call(sum_body, [shape(TOK, wide)] * 3, [], swap(partial, SWAP_AXES)))
 
 
 def solution(mesh):

time: 107 us -> 107 us (level)
  no operation moved by 1% of the time
where the time goes in v4:
time: 107 us; the launch traced here: 106 us
  blocking collectives  61.7 us (58%)
  starting transfers between devices  16.6 us (16%)
  Pallas kernels  13.3 us (12%)
  waiting for transfers between devices  10.5 us (10%)
  local copies, waits for them, and re-layouts  3.35 us (3%)
    all_to_all x3, blocking collectives, swap(): return lax.all_to_all(piece, axes, split_axis=0, concat_axis=0, tiled=True)  61.7 us
    pallas_call x8, Pallas kernels, call(): pl.pallas_call(body, out_shape=out_shapes, in_specs=[pl.BlockSpec(memory_...  13.3 us
    all_to_all x1, starting transfers between devices, swap(): return lax.all_to_all(piece, axes, split_axis=0, concat_axis=0, tiled=True)  12.7 us
    all_to_all x1, waiting for transfers between devices, swap(): return lax.all_to_all(piece, axes, split_axis=0, concat_axis=0, tiled=True)  6.93 us
    ppermute x2, starting transfers between devices, meet(): return lax.ppermute(piece, 'core', [(0, 1), (1, 0)])  3.84 us
    ppermute x2, waiting for transfers between devices, meet(): return lax.ppermute(piece, 'core', [(0, 1), (1, 0)])  3.56 us
    unnamed x8, local copies, waits for them, and re-layouts  3.35 us
  transfers between devices with their start and end apart: 3, of which 3 were waited for; matrix products, arithmetic and copies ran while one was open for 0% of the time, Pallas kernels for 1%

profile of v4, /device:TPU:8, one launch (start us, length us, event | category | flops | bytes accessed | tf_op | source)
XLA Modules:
  0.0 106.2 jit_solution(11804840097599093312)
XLA Ops:
  0.6 0.0 copy-start
  0.6 0.8 copy-done
  1.5 0.6 shard_map.67
  2.1 12.7 %all-to-all-start = ((bf16[8,16,256]{2,1,0:T(8,128)(2,1)}), bf16[8,16,256]{2,1,0:T(8,128)(2,1)S(1)}, u32[]{:S(2)}, u32[]{:S(2)}) async-start(bf16[8,16,256]{2,1,0:T(8,128)(2,1)} %shard_map.67), calls=%async_computation | async-start | bytes 131072 | tf_op jit(solution)/shard_map/all_to_all | solution.py:285
  14.8 0.1 pad_add_fusion.at
  14.9 0.0 copy-start.1
  14.9 0.8 copy-done.1
  15.8 0.0 copy-start.2
  15.8 0.8 copy-done.2
  16.6 0.0 copy-start.3
  16.6 0.8 copy-done.3
  17.4 0.7 shard_map.68.part_ref
  18.2 6.9 %all-to-all-done = bf16[8,16,256]{2,1,0:T(8,128)(2,1)S(1)} async-done(((bf16[8,16,256]{2,1,0:T(8,128)(2,1)}), bf16[8,16,256]{2,1,0:T(8,128)(2,1)S(1)}, u32[]{:S(2)}, u32[]{:S(2)}) %all-to-all-start) | async-done | bytes 65568 | tf_op jit(solution)/shard_map/all_to_all | solution.py:285
  25.1 0.7 shard_map.69
  25.8 31.9 %all_to_all.20.data = bf16[32,96,128]{2,1,0:T(8,128)(2,1)S(1)} all-to-all(bf16[32,96,128]{2,1,0:T(8,128)(2,1)S(1)} %shard_map.69), channel_id=1, replica_groups=mesh['b'=4,'c1'=2,'r1'=2,'c0'=2,'core'=2,'head'=8] {'r1','c0','b','c1'}, dimensions={0} | all-to-all | bytes 1572864 | tf_op jit(solution)/shard_map/all_to_all | solution.py:285
  57.8 1.9 %collective-permute-start = (bf16[32,64,128]{2,1,0:T(8,128)(2,1)S(1)}, bf16[32,64,128]{2,1,0:T(8,128)(2,1)S(1)}, u32[]{:S(2)}, u32[]{:S(2)}) collective-permute-start(bf16[32,64,128]{2,1,0:T(8,128)(2,1)S(1)} %shard_map.70), channel_id=1, source_target_pairs={{0,8},{8,0},{1,9},{9,1},{2,10},{10,2},{3,11},{11,3},{4,12},{12,4},... | collective-permute-start | bytes 1572872 | tf_op jit(solution)/shard_map/ppermute | solution.py:289
  59.7 1.9 %collective-permute-done.other = bf16[32,64,128]{2,1,0:T(8,128)(2,1)S(1)} collective-permute-done((bf16[32,64,128]{2,1,0:T(8,128)(2,1)S(1)}, bf16[32,64,128]{2,1,0:T(8,128)(2,1)S(1)}, u32[]{:S(2)}, u32[]{:S(2)}) %collective-permute-start) | collective-permute-done | bytes 524320 | tf_op jit(solution)/shard_map/ppermute | solution.py:289
  61.6 5.4 %shard_map.71 = (f32[4,8,512]{2,1,0:T(8,128)S(1)}, f32[6,512,512]{2,1,0:T(8,128)S(1)}, f32[4,256,512]{2,1,0:T(8,128)S(1)}, f32[4,256,256]{2,1,0:T(8,128)S(1)}, f...) custom-call(s32[3]{0:T(128)S(1)} %pad_add_fusion.at, ...), custom_call_target="tpu_custom_call" | custom-call | flops 5000000000 | bytes 1048576 | tf_op jit(solution)/shard_map/pallas_call | solution.py:41
  67.0 7.1 %all_to_all.21.stats = f32[4,8,512]{2,1,0:T(8,128)S(1)} all-to-all(f32[4,8,512]{2,1,0:T(8,128)S(1)} %get-tuple-element.13), channel_id=1, replica_groups=mesh['b'=4,'c1'=2,'r1'=2,'c0'=2,'core'=2,'head'=8] {'c1','c0'}, dimensions={0} | all-to-all | bytes 131072 | tf_op jit(solution)/shard_map/all_to_all | solution.py:285
  74.1 4.2 %shard_map.72 = (bf16[32,32,128]{2,1,0:T(8,128)(2,1)S(1)}, bf16[32,16,128]{2,1,0:T(8,128)(2,1)S(1)}, bf16[32,48,128]{2,1,0:T(8,128)(2,1)S(1)}) custom-call(bf16[32,96,128]{2,1,0:T(8,128)(2,1)S(1)} %all_to_all.20.data, bf16[32,64,128]{2,1,0:T(8,128)(2,1)S(1)} %collective-permute-done.other, f32[4,8,512]{2,1,0:T(8,128)S(1)} %all_to_all.21.stats, ...), custom_call_target="tpu_custom_call" | custom-call | flops 7000000000 | bytes 1048576 | tf_op jit(solution)/shard_map/pallas_call | solution.py:41
  78.3 1.9 %collective-permute-start.1 = (bf16[32,48,128]{2,1,0:T(8,128)(2,1)S(1)}, bf16[32,48,128]{2,1,0:T(8,128)(2,1)S(1)}, u32[]{:S(2)}, u32[]{:S(2)}) collective-permute-start(bf16[32,48,128]{2,1,0:T(8,128)(2,1)S(1)} %get-tuple-element.22), channel_id=1, source_target_pairs={{0,8},{8,0},{1,9},{9,1},{2,10},{10,2},{3,11},{11,3},{4,12},{12,4},... | collective-permute-start | bytes 1179656 | tf_op jit(solution)/shard_map/ppermute | solution.py:289
  80.3 1.7 %collective-permute-done.1.got = bf16[32,48,128]{2,1,0:T(8,128)(2,1)S(1)} collective-permute-done((bf16[32,48,128]{2,1,0:T(8,128)(2,1)S(1)}, bf16[32,48,128]{2,1,0:T(8,128)(2,1)S(1)}, u32[]{:S(2)}, u32[]{:S(2)}) %collective-permute-start.1) | collective-permute-done | bytes 393248 | tf_op jit(solution)/shard_map/ppermute | solution.py:289
  81.9 0.6 shard_map.73
  82.6 22.8 %all_to_all.22.part = bf16[32,64,128]{2,1,0:T(8,128)(2,1)S(1)} all-to-all(bf16[32,64,128]{2,1,0:T(8,128)(2,1)S(1)} %shard_map.73), channel_id=1, replica_groups=mesh['b'=4,'c1'=2,'r1'=2,'c0'=2,'core'=2,'head'=8] {'r1','c0','b','c1'}, dimensions={0} | all-to-all | bytes 1048576 | tf_op jit(solution)/shard_map/all_to_all | solution.py:285
  105.4 0.8 shard_map.74
  (1 shorter events, 0.0 us)
Async XLA Ops:
  0.6 0.8 copy-start
  2.1 23.0 %all-to-all-start = ((bf16[8,16,256]{2,1,0:T(8,128)(2,1)}), bf16[8,16,256]{2,1,0:T(8,128)(2,1)S(1)}, u32[]{:S(2)}, u32[]{:S(2)}) async-start(bf16[8,16,256]{2,1,0:T(8,128)(2,1)} %shard_map.67), calls=%async_computation | async-start | bytes 131072 | tf_op jit(solution)/shard_map/all_to_all | solution.py:285
  14.9 0.8 copy-start.1
  15.8 0.8 copy-start.2
  16.6 0.8 copy-start.3
  57.8 3.8 %collective-permute-start = (bf16[32,64,128]{2,1,0:T(8,128)(2,1)S(1)}, bf16[32,64,128]{2,1,0:T(8,128)(2,1)S(1)}, u32[]{:S(2)}, u32[]{:S(2)}) collective-permute-start(bf16[32,64,128]{2,1,0:T(8,128)(2,1)S(1)} %shard_map.70), channel_id=1, source_target_pairs={{0,8},{8,0},{1,9},{9,1},{2,10},{10,2},{3,11},{11,3},{4,12},{12,4},... | collective-permute-start | bytes 1572872 | tf_op jit(solution)/shard_map/ppermute | solution.py:289
  78.3 3.6 %collective-permute-start.1 = (bf16[32,48,128]{2,1,0:T(8,128)(2,1)S(1)}, bf16[32,48,128]{2,1,0:T(8,128)(2,1)S(1)}, u32[]{:S(2)}, u32[]{:S(2)}) collective-permute-start(bf16[32,48,128]{2,1,0:T(8,128)(2,1)S(1)} %get-tuple-element.22), channel_id=1, source_target_pairs={{0,8},{8,0},{1,9},{9,1},{2,10},{10,2},{3,11},{11,3},{4,12},{12,4},... | collective-permute-start | bytes 1179656 | tf_op jit(solution)/shard_map/ppermute | solution.py:289

commit v5 on v2

--- a/solution.py
+++ b/solution.py
@@ -51,9 +51,16 @@
     return jax.ShapeDtypeStruct(dims, dtype)
 
 
-def split_grad(grad, out_ref):
-    for g in range(HEADS):
-        out_ref[g] = grad[:, g * GROUP * D_HEAD : (g + 1) * GROUP * D_HEAD]
+def split_grad(grad, out_ref, sems):
+    wide = GROUP * D_HEAD
+    copies = [
+        pltpu.make_async_copy(grad.at[:, pl.ds(g * wide, wide)], out_ref.at[g], sems.at[g])
+        for g in range(HEADS)
+    ]
+    for copy in copies:
+        copy.start()
+    for copy in copies:
+        copy.wait()
 
 
 def pack_body(at, q_ref, k_ref, v_ref, out_ref, stage):
@@ -290,7 +297,14 @@
     c = 2 * lax.axis_index("c1") + lax.axis_index("c0")
     at = jnp.stack([r, c, core]).astype(jnp.int32)
     wide = GROUP * D_HEAD
-    grad_parts = call(split_grad, shape(HEADS, TOK // HEADS, wide), [], out_grad)
+    grad_parts = pl.pallas_call(
+        split_grad,
+        out_shape=shape(HEADS, TOK // HEADS, wide),
+        in_specs=[pl.BlockSpec(memory_space=pl.ANY)],
+        out_specs=pl.BlockSpec(memory_space=pl.ANY),
+        scratch_shapes=[pltpu.SemaphoreType.DMA((HEADS,))],
+        compiler_params=pltpu.CompilerParams(vmem_limit_bytes=60 * 2**20),
+    )(out_grad)
     grad_local = swap(grad_parts, "head").reshape(TOK, wide)
     message = shape(CHIPS, 3 * PART, 2 * D_HEAD)
     stage = [pltpu.VMEM((GROUP, PART, 2 * D_HEAD), BF)]

time: 107 us -> 108 us (level)
  Pallas kernels: 13.2 us -> 15.5 us
    pallas_call x0 -> x1, Pallas kernels: none -> 3.16 us  [shards(): pl.pallas_call(split_grad, out_shape=shape(HEADS, TOK // HEADS, wide), in...]
    pallas_call x8 -> x7, Pallas kernels: 13.2 us -> 12.4 us  [call(): pl.pallas_call(body, out_shape=out_shapes, in_specs=[pl.BlockSpec(memory_...]
    unnamed x8 -> x6, local copies, waits for them, and re-layouts: 3.35 us -> 2.52 us
where the time goes in v5:
time: 108 us
  blocking collectives  61.9 us (57%)
  starting transfers between devices  16.6 us (15%)
  Pallas kernels  15.5 us (14%)
  waiting for transfers between devices  10.5 us (10%)
  local copies, waits for them, and re-layouts  2.52 us (2%)
    all_to_all x3, blocking collectives, swap(): return lax.all_to_all(piece, axes, split_axis=0, concat_axis=0, tiled=True)  61.9 us
    all_to_all x1, starting transfers between devices, swap(): return lax.all_to_all(piece, axes, split_axis=0, concat_axis=0, tiled=True)  12.8 us
    pallas_call x7, Pallas kernels, call(): pl.pallas_call(body, out_shape=out_shapes, in_specs=[pl.BlockSpec(memory_...  12.4 us
    all_to_all x1, waiting for transfers between devices, swap(): return lax.all_to_all(piece, axes, split_axis=0, concat_axis=0, tiled=True)  6.93 us
    ppermute x2, starting transfers between devices, meet(): return lax.ppermute(piece, 'core', [(0, 1), (1, 0)])  3.84 us
    ppermute x2, waiting for transfers between devices, meet(): return lax.ppermute(piece, 'core', [(0, 1), (1, 0)])  3.56 us
    pallas_call x1, Pallas kernels, shards(): pl.pallas_call(split_grad, out_shape=shape(HEADS, TOK // HEADS, wide), in...  3.16 us
    unnamed x6, local copies, waits for them, and re-layouts  2.52 us
  transfers between devices with their start and end apart: 3, of which 3 were waited for; matrix products, arithmetic and copies ran while one was open for 0% of the time, Pallas kernels for 1%

profile of v5, /device:TPU:8, one launch (start us, length us, event | category | flops | bytes accessed | tf_op | source)
XLA Modules:
  0.0 107.8 jit_solution(14582036783501794457)
XLA Ops:
  0.6 3.2 %shard_map.67 = bf16[8,16,256]{2,1,0:T(8,128)(2,1)} custom-call(bf16[16,2048]{1,0:T(8,128)(2,1)} %grad.1), custom_call_target="tpu_custom_call" | custom-call | tf_op jit(solution)/shard_map/pallas_call | solution.py:300
  3.8 12.8 %all-to-all-start = ((bf16[8,16,256]{2,1,0:T(8,128)(2,1)}), bf16[8,16,256]{2,1,0:T(8,128)(2,1)S(1)}, u32[]{:S(2)}, u32[]{:S(2)}) async-start(bf16[8,16,256]{2,1,0:T(8,128)(2,1)} %shard_map.67), calls=%async_computation | async-start | bytes 131072 | tf_op jit(solution)/shard_map/all_to_all | solution.py:287
  16.6 0.1 pad_add_fusion.at
  16.6 0.0 copy-start
  16.6 0.8 copy-done
  17.5 0.0 copy-start.1
  17.5 0.8 copy-done.1
  18.3 0.0 copy-start.2
  18.3 0.8 copy-done.2
  19.2 0.7 shard_map.68.part_ref
  19.9 6.9 %all-to-all-done = bf16[8,16,256]{2,1,0:T(8,128)(2,1)S(1)} async-done(((bf16[8,16,256]{2,1,0:T(8,128)(2,1)}), bf16[8,16,256]{2,1,0:T(8,128)(2,1)S(1)}, u32[]{:S(2)}, u32[]{:S(2)}) %all-to-all-start) | async-done | bytes 65568 | tf_op jit(solution)/shard_map/all_to_all | solution.py:287
  26.8 0.7 shard_map.69
  27.6 31.8 %all_to_all.20.data = bf16[32,96,128]{2,1,0:T(8,128)(2,1)S(1)} all-to-all(bf16[32,96,128]{2,1,0:T(8,128)(2,1)S(1)} %shard_map.69), channel_id=1, replica_groups=mesh['b'=4,'c1'=2,'r1'=2,'c0'=2,'core'=2,'head'=8] {'b','c1','r1','c0'}, dimensions={0} | all-to-all | bytes 1572864 | tf_op jit(solution)/shard_map/all_to_all | solution.py:287
  59.3 1.9 %collective-permute-start = (bf16[32,64,128]{2,1,0:T(8,128)(2,1)S(1)}, bf16[32,64,128]{2,1,0:T(8,128)(2,1)S(1)}, u32[]{:S(2)}, u32[]{:S(2)}) collective-permute-start(bf16[32,64,128]{2,1,0:T(8,128)(2,1)S(1)} %shard_map.70), channel_id=1, source_target_pairs={{0,8},{8,0},{1,9},{9,1},{2,10},{10,2},{3,11},{11,3},{4,12},{12,4},... | collective-permute-start | bytes 1572872 | tf_op jit(solution)/shard_map/ppermute | solution.py:291
  61.3 1.9 %collective-permute-done.other = bf16[32,64,128]{2,1,0:T(8,128)(2,1)S(1)} collective-permute-done((bf16[32,64,128]{2,1,0:T(8,128)(2,1)S(1)}, bf16[32,64,128]{2,1,0:T(8,128)(2,1)S(1)}, u32[]{:S(2)}, u32[]{:S(2)}) %collective-permute-start) | collective-permute-done | bytes 524320 | tf_op jit(solution)/shard_map/ppermute | solution.py:291
  63.2 5.3 %shard_map.71 = (f32[4,8,512]{2,1,0:T(8,128)S(1)}, f32[6,512,512]{2,1,0:T(8,128)S(1)}, f32[4,256,512]{2,1,0:T(8,128)S(1)}, f32[4,256,256]{2,1,0:T(8,128)S(1)}, f...) custom-call(s32[3]{0:T(128)S(1)} %pad_add_fusion.at, ...), custom_call_target="tpu_custom_call" | custom-call | flops 5000000000 | bytes 1048576 | tf_op jit(solution)/shard_map/pallas_call | solution.py:37
  68.5 7.0 %all_to_all.21.stats = f32[4,8,512]{2,1,0:T(8,128)S(1)} all-to-all(f32[4,8,512]{2,1,0:T(8,128)S(1)} %get-tuple-element.13), channel_id=1, replica_groups=mesh['b'=4,'c1'=2,'r1'=2,'c0'=2,'core'=2,'head'=8] {'c1','c0'}, dimensions={0} | all-to-all | bytes 131072 | tf_op jit(solution)/shard_map/all_to_all | solution.py:287
  75.5 4.1 %shard_map.72 = (bf16[32,32,128]{2,1,0:T(8,128)(2,1)S(1)}, bf16[32,16,128]{2,1,0:T(8,128)(2,1)S(1)}, bf16[32,48,128]{2,1,0:T(8,128)(2,1)S(1)}) custom-call(bf16[32,96,128]{2,1,0:T(8,128)(2,1)S(1)} %all_to_all.20.data, bf16[32,64,128]{2,1,0:T(8,128)(2,1)S(1)} %collective-permute-done.other, f32[4,8,512]{2,1,0:T(8,128)S(1)} %all_to_all.21.stats, ...), custom_call_target="tpu_custom_call" | custom-call | flops 7000000000 | bytes 1048576 | tf_op jit(solution)/shard_map/pallas_call | solution.py:37
  79.6 1.9 %collective-permute-start.1 = (bf16[32,48,128]{2,1,0:T(8,128)(2,1)S(1)}, bf16[32,48,128]{2,1,0:T(8,128)(2,1)S(1)}, u32[]{:S(2)}, u32[]{:S(2)}) collective-permute-start(bf16[32,48,128]{2,1,0:T(8,128)(2,1)S(1)} %get-tuple-element.22), channel_id=1, source_target_pairs={{0,8},{8,0},{1,9},{9,1},{2,10},{10,2},{3,11},{11,3},{4,12},{12,4},... | collective-permute-start | bytes 1179656 | tf_op jit(solution)/shard_map/ppermute | solution.py:291
  81.6 1.7 %collective-permute-done.1.got = bf16[32,48,128]{2,1,0:T(8,128)(2,1)S(1)} collective-permute-done((bf16[32,48,128]{2,1,0:T(8,128)(2,1)S(1)}, bf16[32,48,128]{2,1,0:T(8,128)(2,1)S(1)}, u32[]{:S(2)}, u32[]{:S(2)}) %collective-permute-start.1) | collective-permute-done | bytes 393248 | tf_op jit(solution)/shard_map/ppermute | solution.py:291
  83.3 0.6 shard_map.73
  83.9 23.1 %all_to_all.22.part = bf16[32,64,128]{2,1,0:T(8,128)(2,1)S(1)} all-to-all(bf16[32,64,128]{2,1,0:T(8,128)(2,1)S(1)} %shard_map.73), channel_id=1, replica_groups=mesh['b'=4,'c1'=2,'r1'=2,'c0'=2,'core'=2,'head'=8] {'b','c1','r1','c0'}, dimensions={0} | all-to-all | bytes 1048576 | tf_op jit(solution)/shard_map/all_to_all | solution.py:287
  107.0 0.8 shard_map.74
  (1 shorter events, 0.0 us)
Async XLA Ops:
  3.8 23.0 %all-to-all-start = ((bf16[8,16,256]{2,1,0:T(8,128)(2,1)}), bf16[8,16,256]{2,1,0:T(8,128)(2,1)S(1)}, u32[]{:S(2)}, u32[]{:S(2)}) async-start(bf16[8,16,256]{2,1,0:T(8,128)(2,1)} %shard_map.67), calls=%async_computation | async-start | bytes 131072 | tf_op jit(solution)/shard_map/all_to_all | solution.py:287
  16.6 0.8 copy-start
  17.5 0.8 copy-start.1
  18.3 0.8 copy-start.2
  59.3 3.8 %collective-permute-start = (bf16[32,64,128]{2,1,0:T(8,128)(2,1)S(1)}, bf16[32,64,128]{2,1,0:T(8,128)(2,1)S(1)}, u32[]{:S(2)}, u32[]{:S(2)}) collective-permute-start(bf16[32,64,128]{2,1,0:T(8,128)(2,1)S(1)} %shard_map.70), channel_id=1, source_target_pairs={{0,8},{8,0},{1,9},{9,1},{2,10},{10,2},{3,11},{11,3},{4,12},{12,4},... | collective-permute-start | bytes 1572872 | tf_op jit(solution)/shard_map/ppermute | solution.py:291
  79.6 3.6 %collective-permute-start.1 = (bf16[32,48,128]{2,1,0:T(8,128)(2,1)S(1)}, bf16[32,48,128]{2,1,0:T(8,128)(2,1)S(1)}, u32[]{:S(2)}, u32[]{:S(2)}) collective-permute-start(bf16[32,48,128]{2,1,0:T(8,128)(2,1)S(1)} %get-tuple-element.22), channel_id=1, source_target_pairs={{0,8},{8,0},{1,9},{9,1},{2,10},{10,2},{3,11},{11,3},{4,12},{12,4},... | collective-permute-start | bytes 1179656 | tf_op jit(solution)/shard_map/ppermute | solution.py:291
